TPU v7x, 32 devices: a whole 2x2x4 slice. The times are simulated.
32 devices in a mesh: dp: 8 (over z, x), seq: 4 (over y, core).
Axes of the slice: x: 2, y: 2, z: 4, core: 2. Of those that a mesh axis runs over, the one named last changes fastest.
Arguments:
- tokens: bfloat16 [16384, 768], P(('dp', 'seq')), may hold values from -6 to 6
- cotangent: bfloat16 [16384, 768], P(('dp', 'seq')), may hold values from -6 to 6
- norm_gain: bfloat16 [2, 2, 768], P(None, None, ('dp', 'seq')), may hold values from 0.5 to 1.5
- norm_shift: bfloat16 [2, 2, 768], P(None, None, ('dp', 'seq')), may hold values from -1.796875 to 1.796875
- mixing_weight: bfloat16 [2, 768, 2304], P(None, ('dp', 'seq')), may hold values from -0.21875 to 0.21875
- mixing_bias: bfloat16 [2, 2, 768], P(None, None, ('dp', 'seq')), may hold values from -1.796875 to 1.796875
- output_weight: bfloat16 [2, 768, 768], P(None, ('dp', 'seq')), may hold values from -1.75 to 1.75
- output_bias: bfloat16 [2, 768], P(None, ('dp', 'seq')), may hold values from -1.796875 to 1.796875
- expand_weight: bfloat16 [2, 768, 3072], P(None, ('dp', 'seq')), may hold values from -0.21875 to 0.21875
- expand_bias: bfloat16 [2, 3072], P(None, ('dp', 'seq')), may hold values from -1.796875 to 1.796875
- reduce_weight: bfloat16 [2, 3072, 768], P(None, ('dp', 'seq')), may hold values from -0.109375 to 0.109375
- reduce_bias: bfloat16 [2, 768], P(None, ('dp', 'seq')), may hold values from -1.796875 to 1.796875
Outputs:
- out_tokens: bfloat16 [16384, 768], P(('dp', 'seq'))
- input_grad: float32 [16384, 768], P(('dp', 'seq'))
- norm_gain_grad: float32 [2, 2, 768], P(None, None, ('dp', 'seq'))
- norm_shift_grad: float32 [2, 2, 768], P(None, None, ('dp', 'seq'))
- mixing_weight_grad: float32 [2, 768, 2304], P(None, ('dp', 'seq'))
- mixing_bias_grad: float32 [2, 2, 768], P(None, None, ('dp', 'seq'))
- output_weight_grad: float32 [2, 768, 768], P(None, ('dp', 'seq'))
- output_bias_grad: float32 [2, 768], P(None, ('dp', 'seq'))
- expand_weight_grad: float32 [2, 768, 3072], P(None, ('dp', 'seq'))
- expand_bias_grad: float32 [2, 3072], P(None, ('dp', 'seq'))
- reduce_weight_grad: float32 [2, 3072, 768], P(None, ('dp', 'seq'))
- reduce_bias_grad: float32 [2, 768], P(None, ('dp', 'seq'))
All inputs are finite; a program needn't handle non-finite values.
Results may differ from a plain program's by a relative error of at most 0.011.
Values may be sent and summed in bfloat16 or wider, within the bound.
A program may use at most 256 MiB of HBM per device.

v0:
```python
import jax
import jax.numpy as jnp
from jax import lax
from jax.sharding import PartitionSpec as P

D = 768
HD = 64
LAYERS = 2


norm_epsilon = 1e-05


def layer_norm(values, gain_row, shift_row):
    center = values - jnp.mean(values, axis=-1, keepdims=True)
    spread = jnp.mean(center * center, axis=-1, keepdims=True)
    return center * lax.rsqrt(spread + norm_epsilon) * gain_row + shift_row


def gelu_tanh(values):
    return jax.nn.gelu(values, approximate=True)


def matmul(left, right):
    return jnp.dot(left, right, preferred_element_type=jnp.float32)


def split_heads(packed):
    length = packed.shape[0]
    groups = packed.shape[3] // HD
    query = packed[:, 0, 0].reshape(length, groups, HD)
    keys = packed[:, 1, 0].reshape(length, groups, HD)
    values = packed[:, 2, 0].reshape(length, groups, HD)
    return (query, keys, values)


def block_scores(query_block, keys, block_index):
    block_rows = query_block.shape[0]
    scores = jnp.einsum(
        "qhd,khd->hqk", query_block, keys, preferred_element_type=jnp.float32
    ) * HD ** (-0.5)
    row_place = block_index * block_rows + jnp.arange(block_rows)
    key_place = jnp.arange(keys.shape[0])
    allowed = key_place[None, :] <= row_place[:, None]
    return jnp.where(allowed[None], scores, -1e30)


def attend_forward(packed):
    query, keys, values = split_heads(packed)
    length, groups = (query.shape[0], query.shape[1])
    block_rows = min(512, length)
    block_count = length // block_rows

    def one_block(item_pack):
        query_block, block_index = item_pack
        scores = block_scores(query_block, keys, block_index)
        peak_score = jnp.max(scores, axis=-1, keepdims=True)
        weights = jnp.exp(scores - peak_score)
        totals = jnp.sum(weights, axis=-1, keepdims=True)
        shares = (weights / totals).astype(jnp.bfloat16)
        attended = jnp.einsum("hqk,khd->qhd", shares, values, preferred_element_type=jnp.float32)
        return (attended.astype(jnp.bfloat16), (peak_score + jnp.log(totals))[..., 0])

    attended, log_totals = lax.map(
        one_block, (query.reshape(block_count, block_rows, groups, HD), jnp.arange(block_count))
    )
    return (attended.reshape(length, groups * HD), log_totals)


def attend_backward(packed, log_totals, grad_rows):
    query, keys, values = split_heads(packed)
    length, groups = (query.shape[0], query.shape[1])
    block_rows = min(512, length)
    block_count = length // block_rows
    scale = HD ** (-0.5)

    def one_block(carried, item_pack):
        key_grad, value_grad = carried
        query_block, grad_block, log_block, block_index = item_pack
        scores = block_scores(query_block, keys, block_index)
        shares = jnp.exp(scores - log_block[:, :, None])
        value_grad = value_grad + jnp.einsum(
            "hqk,qhd->khd",
            shares.astype(jnp.bfloat16),
            grad_block,
            preferred_element_type=jnp.float32,
        )
        share_grad = jnp.einsum(
            "qhd,khd->hqk", grad_block, values, preferred_element_type=jnp.float32
        )
        inner = jnp.sum(shares * share_grad, axis=-1, keepdims=True)
        score_grad = (shares * (share_grad - inner)).astype(jnp.bfloat16)
        query_grad = (
            jnp.einsum("hqk,khd->qhd", score_grad, keys, preferred_element_type=jnp.float32) * scale
        )
        key_grad = (
            key_grad
            + jnp.einsum(
                "hqk,qhd->khd", score_grad, query_block, preferred_element_type=jnp.float32
            )
            * scale
        )
        return ((key_grad, value_grad), query_grad.astype(jnp.bfloat16))

    zeros_state = jnp.zeros((length, groups, HD), jnp.float32)
    item_pack = (
        query.reshape(block_count, block_rows, groups, HD),
        grad_rows.reshape(block_count, block_rows, groups, HD),
        log_totals,
        jnp.arange(block_count),
    )
    (key_grad, value_grad), query_grad = lax.scan(one_block, (zeros_state, zeros_state), item_pack)
    stacked = jnp.stack(
        [
            query_grad.reshape(length, groups * HD),
            key_grad.reshape(length, groups * HD).astype(jnp.bfloat16),
            value_grad.reshape(length, groups * HD).astype(jnp.bfloat16),
        ],
        axis=1,
    )
    return stacked[:, :, None, :]


def body(
    tokens,
    cotangent,
    norm_gain,
    norm_shift,
    mixing_weight,
    mixing_bias,
    output_weight,
    output_bias,
    expand_weight,
    expand_bias,
    reduce_weight,
    reduce_bias,
):
    seq_parts = lax.axis_size("seq")
    local_rows = tokens.shape[0]
    hidden = tokens.astype(jnp.float32)
    saved = []
    for layer_index in range(LAYERS):
        gain_piece = norm_gain[layer_index]
        shift_piece = norm_shift[layer_index]
        mixing_piece = mixing_weight[layer_index]
        mixbias_piece = mixing_bias[layer_index]
        outw_piece = output_weight[layer_index]
        outb_piece = output_bias[layer_index]
        expw_piece = expand_weight[layer_index]
        expb_piece = expand_bias[layer_index]
        redw_piece = reduce_weight[layer_index]
        redb_piece = reduce_bias[layer_index]
        gathered = (
            lax.all_gather(gain_piece, ("dp", "seq"), axis=1, tiled=True),
            lax.all_gather(shift_piece, ("dp", "seq"), axis=1, tiled=True),
            lax.all_gather(mixing_piece, ("dp", "seq"), axis=0, tiled=True),
            lax.all_gather(mixbias_piece, ("dp", "seq"), axis=1, tiled=True),
            lax.all_gather(outw_piece, ("dp", "seq"), axis=0, tiled=True),
            lax.all_gather(outb_piece, ("dp", "seq"), axis=0, tiled=True),
            lax.all_gather(expw_piece, ("dp", "seq"), axis=0, tiled=True),
            lax.all_gather(expb_piece, ("dp", "seq"), axis=0, tiled=True),
            lax.all_gather(redw_piece, ("dp", "seq"), axis=0, tiled=True),
            lax.all_gather(redb_piece, ("dp", "seq"), axis=0, tiled=True),
        )
        gains = gathered[0].astype(jnp.float32)
        shifts = gathered[1].astype(jnp.float32)
        normed = layer_norm(hidden, gains[0], shifts[0]).astype(jnp.bfloat16)
        bias_row = jnp.concatenate(
            [gathered[3][0], jnp.zeros((D,), jnp.bfloat16), gathered[3][1]]
        ).astype(jnp.float32)
        mixed_rows = (matmul(normed, gathered[2]) + bias_row).astype(jnp.bfloat16)
        packed = lax.all_to_all(
            mixed_rows.reshape(local_rows, 3, seq_parts, -1),
            "seq",
            split_axis=2,
            concat_axis=0,
            tiled=True,
        )
        attended, log_totals = attend_forward(packed)
        returned = lax.all_to_all(
            attended.reshape(attended.shape[0], 1, -1),
            "seq",
            split_axis=0,
            concat_axis=1,
            tiled=True,
        )
        merged = returned.reshape(local_rows, D)
        middle = hidden + (matmul(merged, gathered[4]) + gathered[5].astype(jnp.float32))
        normed_two = layer_norm(middle, gains[1], shifts[1]).astype(jnp.bfloat16)
        pre_gelu = matmul(normed_two, gathered[6]) + gathered[7].astype(jnp.float32)
        activated = gelu_tanh(pre_gelu).astype(jnp.bfloat16)
        saved.append(
            (
                hidden,
                normed,
                packed,
                log_totals,
                merged,
                middle,
                normed_two,
                pre_gelu,
                activated,
                gathered,
            )
        )
        hidden = middle + (matmul(activated, gathered[8]) + gathered[9].astype(jnp.float32))
    out_tokens = hidden.astype(jnp.bfloat16)
    running_grad = cotangent.astype(jnp.float32)
    shard_lists = []
    for layer_index in reversed(range(LAYERS)):
        (
            layer_input,
            normed,
            packed,
            log_totals,
            merged,
            middle,
            normed_two,
            pre_gelu,
            activated,
            kept_weights,
        ) = saved[layer_index]
        gathered = (
            lax.all_gather(norm_gain[layer_index], ("dp", "seq"), axis=1, tiled=True),
            lax.all_gather(norm_shift[layer_index], ("dp", "seq"), axis=1, tiled=True),
            lax.all_gather(mixing_weight[layer_index], ("dp", "seq"), axis=0, tiled=True),
            lax.all_gather(mixing_bias[layer_index], ("dp", "seq"), axis=1, tiled=True),
            lax.all_gather(output_weight[layer_index], ("dp", "seq"), axis=0, tiled=True),
            lax.all_gather(output_bias[layer_index], ("dp", "seq"), axis=0, tiled=True),
            lax.all_gather(expand_weight[layer_index], ("dp", "seq"), axis=0, tiled=True),
            lax.all_gather(expand_bias[layer_index], ("dp", "seq"), axis=0, tiled=True),
            lax.all_gather(reduce_weight[layer_index], ("dp", "seq"), axis=0, tiled=True),
            lax.all_gather(reduce_bias[layer_index], ("dp", "seq"), axis=0, tiled=True),
        )
        gains = gathered[0].astype(jnp.float32)
        shifts = gathered[1].astype(jnp.float32)
        reduce_bias_grad = jnp.sum(running_grad, axis=0)
        grad_low = running_grad.astype(jnp.bfloat16)
        reduce_weight_grad = jnp.einsum(
            "tf,td->fd", activated, grad_low, preferred_element_type=jnp.float32
        )
        act_grad = jnp.einsum(
            "td,fd->tf", grad_low, gathered[8], preferred_element_type=jnp.float32
        )
        unused_value, gelu_pull = jax.vjp(gelu_tanh, pre_gelu)
        pre_grad = gelu_pull(act_grad)[0].astype(jnp.bfloat16)
        expand_bias_grad = jnp.sum(pre_grad.astype(jnp.float32), axis=0)
        expand_weight_grad = jnp.einsum(
            "td,tf->df", normed_two, pre_grad, preferred_element_type=jnp.float32
        )
        second_in = jnp.einsum(
            "tf,df->td", pre_grad, gathered[6], preferred_element_type=jnp.float32
        )
        unused_norm, norm_pull = jax.vjp(layer_norm, middle, gains[1], shifts[1])
        middle_grad, gain_two, shift_two = norm_pull(second_in)
        running_grad = running_grad + middle_grad
        output_bias_grad = jnp.sum(running_grad, axis=0)
        out_low = running_grad.astype(jnp.bfloat16)
        output_weight_grad = jnp.einsum(
            "ti,td->id", merged, out_low, preferred_element_type=jnp.float32
        )
        merged_grad = jnp.einsum(
            "td,id->ti", out_low, gathered[4], preferred_element_type=jnp.float32
        ).astype(jnp.bfloat16)
        head_grad = lax.all_to_all(
            merged_grad.reshape(local_rows, seq_parts, -1),
            "seq",
            split_axis=1,
            concat_axis=0,
            tiled=True,
        )
        packed_grad = attend_backward(packed, log_totals, head_grad.reshape(head_grad.shape[0], -1))
        mixed_grad = lax.all_to_all(
            packed_grad, "seq", split_axis=0, concat_axis=2, tiled=True
        ).reshape(local_rows, 3 * D)
        mixing_weight_grad = jnp.einsum(
            "td,tc->dc", normed, mixed_grad, preferred_element_type=jnp.float32
        )
        column_sums = jnp.sum(mixed_grad.astype(jnp.float32), axis=0).reshape(3, D)
        mixing_bias_grad = jnp.stack([column_sums[0], column_sums[2]])
        first_in = jnp.einsum(
            "tc,dc->td", mixed_grad, gathered[2], preferred_element_type=jnp.float32
        )
        unused_first, first_pull = jax.vjp(layer_norm, layer_input, gains[0], shifts[0])
        input_part, gain_one, shift_one = first_pull(first_in)
        running_grad = running_grad + input_part
        gain_grads = jnp.stack([gain_one, gain_two])
        shift_grads = jnp.stack([shift_one, shift_two])
        local_grads = (
            gain_grads,
            shift_grads,
            mixing_weight_grad,
            mixing_bias_grad,
            output_weight_grad,
            output_bias_grad,
            expand_weight_grad,
            expand_bias_grad,
            reduce_weight_grad,
            reduce_bias_grad,
        )
        shards = (
            lax.psum_scatter(local_grads[0], ("dp", "seq"), scatter_dimension=1, tiled=True),
            lax.psum_scatter(local_grads[1], ("dp", "seq"), scatter_dimension=1, tiled=True),
            lax.psum_scatter(local_grads[2], ("dp", "seq"), scatter_dimension=0, tiled=True),
            lax.psum_scatter(local_grads[3], ("dp", "seq"), scatter_dimension=1, tiled=True),
            lax.psum_scatter(local_grads[4], ("dp", "seq"), scatter_dimension=0, tiled=True),
            lax.psum_scatter(local_grads[5], ("dp", "seq"), scatter_dimension=0, tiled=True),
            lax.psum_scatter(local_grads[6], ("dp", "seq"), scatter_dimension=0, tiled=True),
            lax.psum_scatter(local_grads[7], ("dp", "seq"), scatter_dimension=0, tiled=True),
            lax.psum_scatter(local_grads[8], ("dp", "seq"), scatter_dimension=0, tiled=True),
            lax.psum_scatter(local_grads[9], ("dp", "seq"), scatter_dimension=0, tiled=True),
        )
        shard_lists.insert(0, shards)
    stacked = tuple(
        (jnp.stack([shard_lists[index][member] for index in range(LAYERS)]) for member in range(10))
    )
    return (
        out_tokens,
        running_grad,
        stacked[0],
        stacked[1],
        stacked[2],
        stacked[3],
        stacked[4],
        stacked[5],
        stacked[6],
        stacked[7],
        stacked[8],
        stacked[9],
    )


def solution(mesh):
    return jax.shard_map(
        body,
        mesh=mesh,
        in_specs=(
            P(("dp", "seq"), None),
            P(("dp", "seq"), None),
            P(None, None, ("dp", "seq")),
            P(None, None, ("dp", "seq")),
            P(None, ("dp", "seq"), None),
            P(None, None, ("dp", "seq")),
            P(None, ("dp", "seq"), None),
            P(None, ("dp", "seq")),
            P(None, ("dp", "seq"), None),
            P(None, ("dp", "seq")),
            P(None, ("dp", "seq"), None),
            P(None, ("dp", "seq")),
        ),
        out_specs=(
            P(("dp", "seq"), None),
            P(("dp", "seq"), None),
            P(None, None, ("dp", "seq")),
            P(None, None, ("dp", "seq")),
            P(None, ("dp", "seq"), None),
            P(None, None, ("dp", "seq")),
            P(None, ("dp", "seq"), None),
            P(None, ("dp", "seq")),
            P(None, ("dp", "seq"), None),
            P(None, ("dp", "seq")),
            P(None, ("dp", "seq"), None),
            P(None, ("dp", "seq")),
        ),
        check_vma=False,
    )
```

profile of v0, /device:TPU:0, one launch (start us, length us, event | category | flops | bytes accessed | tf_op | source)
XLA Modules:
  0.0 2352.6 jit_solution(6295833970513050767)
XLA Ops:
  15.9 44.8 %all-gather.13 = bf16[1,2,768]{1,0,2:T(2,128)(2,1)S(1)} all-gather(bf16[1,2,24]{1,0,2:T(2,128)(2,1)S(1)} %copy.199), channel_id=15, replica_groups=mesh['dp'=8,'seq'=4] {'dp','seq'}, dimensions={2}, use_global_device_ids=true | all-gather | bytes 3168 | tf_op jit(solution)/shard_map/all_gather | solution.py:157
  65.6 37.8 %all-gather.3 = bf16[1,2,768]{1,0,2:T(2,128)(2,1)S(1)} all-gather(bf16[1,2,24]{1,0,2:T(2,128)(2,1)S(1)} %copy.196), channel_id=5, replica_groups=mesh['dp'=8,'seq'=4] {'dp','seq'}, dimensions={2}, use_global_device_ids=true | all-gather | bytes 3168 | tf_op jit(solution)/shard_map/all_gather | solution.py:157
  108.8 39.5 %all-gather.1 = bf16[1,2,768]{1,0,2:T(2,128)(2,1)S(1)} all-gather(bf16[1,2,24]{1,0,2:T(2,128)(2,1)S(1)} %copy.195), channel_id=3, replica_groups=mesh['dp'=8,'seq'=4] {'dp','seq'}, dimensions={2}, use_global_device_ids=true | all-gather | bytes 3168 | tf_op jit(solution)/shard_map/all_gather | solution.py:155
  153.8 38.4 %all-gather = bf16[1,2,768]{1,0,2:T(2,128)(2,1)S(1)} all-gather(bf16[1,2,24]{1,0,2:T(2,128)(2,1)S(1)} %copy.194), channel_id=2, replica_groups=mesh['dp'=8,'seq'=4] {'dp','seq'}, dimensions={2}, use_global_device_ids=true | all-gather | bytes 3168 | tf_op jit(solution)/shard_map/all_gather | solution.py:154
  215.1 28.9 %all-to-all-done = bf16[512,3,4,192]{0,3,1,2:T(8,128)(2,1)S(1)} async-done(((bf16[512,3,4,192]{0,3,1,2:T(8,128)(2,1)}), bf16[512,3,4,192]{0,3,1,2:T(8,128)(2,1)S(1)}, u32[]{:S(2)}, u32[]{:S(2)}) %all-to-all-start) | async-done | bytes 2359328 | tf_op jit(solution)/shard_map/all_to_all | solution.py:172
  245.4 86.4 %while.54 = (s32[]{:T(128)}, bf16[4,512,3,64]{1,3,2,0:T(8,128)(2,1)S(1)}, f32[4,3,512]{2,1,0:T(4,128)S(1)}, s32[4]{0:T(128)S(1)}, bf16[4,512,3,64]{1,3,2,0:T(8,1...) while((s32[]{:T(128)}, ...), condition=%wide.region_5.6_spmd, body=%wide.region_2.5_spmd.sunk | while | flops 844200960 | bytes 43972748 | solution.py:64
  253.4 6.9 fusion.266
  275.1 6.8 fusion.266
  324.9 6.9 fusion.267
  346.6 43.5 %all-reduce.19 = (bf16[768]{0:T(1024)(128)(2,1)S(1)}, bf16[768]{0:T(1024)(128)(2,1)S(1)}, bf16[3072]{0:T(1024)(128)(2,1)S(1)}, bf16[768]{0:T(1024)(128)(2,1)}, b...) all-reduce(bf16[768]{0:T(1024)(128)(2,1)S(1)} %dynamic-update-slice, ...), channel_id=7, replica_groups=mesh['dp'=8,'seq'=4] {'dp','seq'}, use_global_device_ids=true, to_apply=%add | all-reduce | flops 9216 | bytes 36864
  390.2 43.4 %all-gather.11 = bf16[1,2,768]{1,0,2:T(2,128)(2,1)S(1)} all-gather(bf16[1,2,24]{1,0,2:T(2,128)(2,1)S(1)} %copy.198), channel_id=13, replica_groups=mesh['dp'=8,'seq'=4] {'dp','seq'}, dimensions={2}, use_global_device_ids=true | all-gather | bytes 3168 | tf_op jit(solution)/shard_map/all_gather | solution.py:155
  434.2 38.0 %all-gather.10 = bf16[1,2,768]{1,0,2:T(2,128)(2,1)S(1)} all-gather(bf16[1,2,24]{1,0,2:T(2,128)(2,1)S(1)} %copy.197), channel_id=12, replica_groups=mesh['dp'=8,'seq'=4] {'dp','seq'}, dimensions={2}, use_global_device_ids=true | all-gather | bytes 3168 | tf_op jit(solution)/shard_map/all_gather | solution.py:154
  494.2 7.0 fusion.114
  501.3 7.6 fusion.197
  526.5 28.9 %all-to-all-done.2 = bf16[512,3,4,192]{0,3,1,2:T(8,128)(2,1)S(1)} async-done(((bf16[512,3,4,192]{0,3,1,2:T(8,128)(2,1)}), bf16[512,3,4,192]{0,3,1,2:T(8,128)(2,1)S(1)}, u32[]{:S(2)}, u32[]{:S(2)}) %all-to-all-start.2) | async-done | bytes 2359328 | tf_op jit(solution)/shard_map/all_to_all | solution.py:172
  556.7 86.2 %while.55 = (s32[]{:T(128)}, bf16[4,512,3,64]{1,3,2,0:T(8,128)(2,1)S(1)}, f32[4,3,512]{2,1,0:T(4,128)S(1)}, s32[4]{0:T(128)S(1)}, bf16[4,512,3,64]{1,3,2,0:T(8,1...) while((s32[]{:T(128)}, ...), condition=%wide.region_13.14_spmd, body=%wide.region_10.13_spmd.sunk | while | flops 844200960 | bytes 43972748 | solution.py:64
  586.4 6.9 fusion.271
  656.2 11.5 all-to-all-done.3
  682.2 8.3 fusion.106
  690.6 9.8 convert_reduce_fusion
  713.3 11.6 all-to-all-done.4
  725.9 136.4 %while.56 = (s32[]{:T(128)}, f32[2048,3,64]{0,2,1:T(8,128)}, f32[2048,3,64]{0,2,1:T(8,128)}, bf16[4,512,3,64]{1,3,2,0:T(8,128)(2,1)}, bf16[4,512,3,64]{1,3,2,0:T...) while((s32[]{:T(128)}, f32[2048,3,64]{0,2,1:T(8,128)}, ...), condition=%wide.region_20.21_spmd.clone, body=%wide.region_18.20_spmd.clone.sunk | while | flops 2063662080 | bytes 219396720 | solution.py:112
  750.0 6.8 fusion.284
  784.1 6.8 fusion.284
  818.1 6.8 fusion.284
  852.2 6.8 fusion.284
  873.5 53.9 %all_to_all.126 = bf16[2048,3,1,192]{3,1,2,0:T(4,128)(2,1)} all-to-all(bf16[2048,3,1,192]{3,1,2,0:T(4,128)(2,1)} %copy.167), channel_id=1, replica_groups=mesh['dp'=8,'seq'=4] {'seq'}, dimensions={0} | all-to-all | bytes 4718592 | tf_op jit(solution)/shard_map/all_to_all | solution.py:273
  927.3 7.2 copy.180
  945.8 7.2 convert_reduce_fusion.1
  964.7 11.6 all-to-all-done.6
  977.3 140.9 %while.57 = (s32[]{:T(128)}, f32[2048,3,64]{0,2,1:T(8,128)}, f32[2048,3,64]{0,2,1:T(8,128)}, bf16[4,512,3,64]{1,3,2,0:T(8,128)(2,1)}, bf16[4,512,3,64]{1,3,2,0:T...) while((s32[]{:T(128)}, f32[2048,3,64]{0,2,1:T(8,128)}, ...), condition=%wide.region_27.28_spmd.clone, body=%wide.region_25.27_spmd.clone.sunk | while | flops 2063662080 | bytes 203669984 | solution.py:112
  1137.9 44.8 %all-to-all-done.7 = bf16[2048,3,1,192]{3,1,2,0:T(4,128)(2,1)} async-done(((bf16[2048,3,1,192]{3,1,2,0:T(4,128)(2,1)}), bf16[2048,3,1,192]{3,1,2,0:T(4,128)(2,1)}, u32[]{:S(2)}, u32[]{:S(2)}) %all-to-all-start.7) | async-done | bytes 2359328 | tf_op jit(solution)/shard_map/all_to_all | solution.py:273
  1182.7 7.2 copy.181
  1213.7 6.8 fusion.170
  1221.2 8.9 fusion.176
  1230.9 8.8 fusion.174
  1240.9 10.0 fusion.178
  1251.6 10.7 fusion.150
  1262.9 9.6 add_convert_fusion
  1274.2 46.0 %all-reduce.22.cloned.1.call-done = (f32[2,768]{1,0:T(2,128)}, f32[2,768]{1,0:T(2,128)}, f32[2,768]{1,0:T(2,128)}, f32[2,768]{1,0:T(2,128)}, f32[2,768]{1,0:T(2,...) async-done(((f32[2,768]{1,0:T(2,128)}, f32[2,768]{1,0:T(2,128)}, ...) | async-done | bytes 73744
  1328.3 100.0 %reduce-scatter.21.cloned.1.call-done = f32[24,768]{1,0:T(8,128)} async-done(((f32[768,768]{1,0:T(8,128)}), f32[24,768]{1,0:T(8,128)}) %reduce-scatter.21.cloned.1.call-update) | async-done | bytes 73744 | tf_op jit(solution)/shard_map/reduce_scatter | solution.py:306
  1428.3 103.3 %reduce-scatter.19.cloned.1.call-done = f32[24,768]{1,0:T(8,128)} async-done(((f32[768,768]{1,0:T(8,128)}), f32[24,768]{1,0:T(8,128)}) %reduce-scatter.19.cloned.1.call-update) | async-done | bytes 73744 | tf_op jit(solution)/shard_map/reduce_scatter | solution.py:306
  1533.2 123.0 %reduce-scatter.17.cloned.1.call-done = f32[24,2304]{1,0:T(8,128)} async-done(((f32[768,2304]{1,0:T(8,128)}), f32[24,2304]{1,0:T(8,128)}) %reduce-scatter.17.cloned.1.call-update) | async-done | bytes 221200 | tf_op jit(solution)/shard_map/reduce_scatter | solution.py:304
  1656.2 124.1 %reduce-scatter.15.cloned.1.call-done = f32[24,2304]{1,0:T(8,128)} async-done(((f32[768,2304]{1,0:T(8,128)}), f32[24,2304]{1,0:T(8,128)}) %reduce-scatter.15.cloned.1.call-update) | async-done | bytes 221200 | tf_op jit(solution)/shard_map/reduce_scatter | solution.py:304
  1782.1 140.0 %reduce-scatter.25.cloned.1.call-done = f32[24,3072]{1,0:T(8,128)} async-done(((f32[768,3072]{1,0:T(8,128)}), f32[24,3072]{1,0:T(8,128)}) %reduce-scatter.25.cloned.1.call-update) | async-done | bytes 294928 | tf_op jit(solution)/shard_map/reduce_scatter | solution.py:308
  1922.0 140.3 %reduce-scatter.23.cloned.1.call-done = f32[24,3072]{1,0:T(8,128)} async-done(((f32[768,3072]{1,0:T(8,128)}), f32[24,3072]{1,0:T(8,128)}) %reduce-scatter.23.cloned.1.call-update) | async-done | bytes 294928 | tf_op jit(solution)/shard_map/reduce_scatter | solution.py:308
  2064.3 139.4 %reduce-scatter.29.cloned.1.call-done = f32[96,768]{1,0:T(8,128)} async-done(((f32[3072,768]{1,0:T(8,128)}), f32[96,768]{1,0:T(8,128)}) %reduce-scatter.29.cloned.1.call-update) | async-done | bytes 294928 | tf_op jit(solution)/shard_map/reduce_scatter | solution.py:310
  2203.7 140.3 %reduce-scatter.27.cloned.1.call-done = f32[96,768]{1,0:T(8,128)} async-done(((f32[3072,768]{1,0:T(8,128)}), f32[96,768]{1,0:T(8,128)}) %reduce-scatter.27.cloned.1.call-update) | async-done | bytes 294928 | tf_op jit(solution)/shard_map/reduce_scatter | solution.py:310
  (799 shorter events, 626.2 us)
Async XLA Ops:
  7.2 101.0 %copy-start.123 = (bf16[2,2,24]{2,1,0:T(2,128)(2,1)S(1)}, bf16[2,2,24]{2,1,0:T(2,128)(2,1)}, u32[]{:S(2)}) copy-start(bf16[2,2,24]{2,1,0:T(2,128)(2,1)} %param.23) | copy-start | bytes 580
  7.2 191.8 %all-gather.29.cloned.1.call-start = ((), (), s32[]{:S(2)}) async-start(), calls=%async_computation.24 | async-start | bytes 3649536 | tf_op jit(solution)/shard_map/all_gather | solution.py:156
  8.9 144.3 %copy-start.124 = (bf16[2,2,24]{2,1,0:T(2,128)(2,1)S(1)}, bf16[2,2,24]{2,1,0:T(2,128)(2,1)}, u32[]{:S(2)}) copy-start(bf16[2,2,24]{2,1,0:T(2,128)(2,1)} %param.22) | copy-start | bytes 580
  8.9 481.7 %all-gather.31.cloned.1.call-start = ((), (), s32[]{:S(2)}) async-start(), calls=%async_computation.25 | async-start | bytes 1216512 | tf_op jit(solution)/shard_map/all_gather | solution.py:158
  10.4 483.1 %all-gather.33.cloned.1.call-start = ((), (), s32[]{:S(2)}) async-start(), calls=%async_computation.26 | async-start | bytes 4866048 | tf_op jit(solution)/shard_map/all_gather | solution.py:160
  12.2 489.1 %all-gather.35.cloned.1.call-start = ((), (), s32[]{:S(2)}) async-start(), calls=%async_computation.27 | async-start | bytes 4866048 | tf_op jit(solution)/shard_map/all_gather | solution.py:162
  14.0 496.9 %all-gather.37.cloned.1.call-start = ((), (), s32[]{:S(2)}) async-start(), calls=%async_computation.28 | async-start | bytes 3649536 | tf_op jit(solution)/shard_map/all_gather | solution.py:156
  14.6 663.1 %all-gather.39.cloned.1.call-start = ((), (), s32[]{:S(2)}) async-start(), calls=%async_computation.29 | async-start | bytes 1216512 | tf_op jit(solution)/shard_map/all_gather | solution.py:158
  15.9 181.3 %copy-start.21 = (bf16[512,768]{1,0:T(8,128)(2,1)S(1)}, bf16[512,768]{1,0:T(8,128)(2,1)}, u32[]{:S(2)}) copy-start(bf16[512,768]{1,0:T(8,128)(2,1)} %param.20) | copy-start | bytes 2359300
  153.2 45.8 %copy-start.104 = (f32[768]{0:T(1024)}, f32[768]{0:T(1024)S(1)}, u32[]{:S(2)}) copy-start(f32[768]{0:T(1024)S(1)} %get-tuple-element.466) | copy-start | bytes 9220
  209.7 34.3 %all-to-all-start = ((bf16[512,3,4,192]{0,3,1,2:T(8,128)(2,1)}), bf16[512,3,4,192]{0,3,1,2:T(8,128)(2,1)S(1)}, u32[]{:S(2)}, u32[]{:S(2)}) async-start(bf16[512,3,4,192]{0,3,1,2:T(8,128)(2,1)} %copy.146), calls=%async_computation | async-start | bytes 4718592 | tf_op jit(solution)/shard_map/all_to_all | solution.py:172
  213.4 468.7 %all-gather.41.cloned.1.call-start = ((), (), s32[]{:S(2)}) async-start(), calls=%async_computation.30 | async-start | bytes 4866048 | tf_op jit(solution)/shard_map/all_gather | solution.py:160
  336.1 54.0 %copy-start.121 = (bf16[1,2,24]{2,1,0:T(2,128)(2,1)S(1)}, bf16[1,2,24]{2,1,0:T(2,128)(2,1)}, u32[]{:S(2)}) copy-start(bf16[1,2,24]{2,1,0:T(2,128)(2,1)} %get-tuple-element.597) | copy-start | bytes 292
  338.0 96.0 %copy-start.122 = (bf16[1,2,24]{2,1,0:T(2,128)(2,1)S(1)}, bf16[1,2,24]{2,1,0:T(2,128)(2,1)}, u32[]{:S(2)}) copy-start(bf16[1,2,24]{2,1,0:T(2,128)(2,1)} %get-tuple-element.595) | copy-start | bytes 292
  341.9 139.9 %all-to-all-start.1 = ((bf16[4,2,49152]{2,1,0:T(2,128)(2,1)}), bf16[4,2,49152]{2,1,0:T(2,128)(2,1)}, u32[]{:S(2)}, u32[]{:S(2)}) async-start(bf16[4,2,49152]{2,1,0:T(2,128)(2,1)} %reshape.572), calls=%async_computation.1 | async-start | bytes 1572864 | tf_op jit(solution)/shard_map/all_to_all | solution.py:180
  390.1 111.2 %copy-start.87 = (f32[3072]{0:T(1024)}, f32[3072]{0:T(1024)S(1)}, u32[]{:S(2)}) copy-start(f32[3072]{0:T(1024)S(1)} %convert_element_type.262) | copy-start | bytes 36868
  477.2 33.8 %copy-start.108 = (f32[768]{0:T(1024)}, f32[768]{0:T(1024)S(1)}, u32[]{:S(2)}) copy-start(f32[768]{0:T(1024)S(1)} %get-tuple-element.460) | copy-start | bytes 9220
  481.7 29.2 %copy-start.84 = (f32[768]{0:T(1024)}, f32[768]{0:T(1024)S(1)}, u32[]{:S(2)}) copy-start(f32[768]{0:T(1024)S(1)} %get-tuple-element.458) | copy-start | bytes 9220
  522.1 33.3 %all-to-all-start.2 = ((bf16[512,3,4,192]{0,3,1,2:T(8,128)(2,1)}), bf16[512,3,4,192]{0,3,1,2:T(8,128)(2,1)S(1)}, u32[]{:S(2)}, u32[]{:S(2)}) async-start(bf16[512,3,4,192]{0,3,1,2:T(8,128)(2,1)} %copy.157), calls=%async_computation.2 | async-start | bytes 4718592 | tf_op jit(solution)/shard_map/all_to_all | solution.py:172
  525.7 164.8 %all-gather.43.cloned.1.call-start = ((), (), s32[]{:S(2)}) async-start(), calls=%async_computation.31 | async-start | bytes 4866048 | tf_op jit(solution)/shard_map/all_gather | solution.py:162
  652.3 15.5 all-to-all-start.3
  656.2 34.3 %copy-start.90 = (f32[3072]{0:T(1024)}, f32[3072]{0:T(1024)S(1)}, u32[]{:S(2)}) copy-start(f32[3072]{0:T(1024)S(1)} %convert_element_type.265) | copy-start | bytes 36868
  680.6 23.2 copy-start.71
  682.2 21.7 copy-start.99
  709.8 15.1 all-to-all-start.4
  744.5 12.3 slice-start
  778.1 12.8 slice-start
  812.2 12.8 slice-start
  846.3 12.8 slice-start
  934.6 11.1 slice-start.6
  934.6 11.1 slice-start.8
  945.7 11.5 copy-start.28
  959.2 18.1 copy-start.5
  961.2 15.1 all-to-all-start.6
  997.3 12.3 slice-start.2
  1032.1 12.7 slice-start.2
  1067.3 12.7 slice-start.2
  1102.5 12.7 slice-start.2
  1129.5 53.2 %all-to-all-start.7 = ((bf16[2048,3,1,192]{3,1,2,0:T(4,128)(2,1)}), bf16[2048,3,1,192]{3,1,2,0:T(4,128)(2,1)}, u32[]{:S(2)}, u32[]{:S(2)}) async-start(bf16[2048,3,1,192]{3,1,2,0:T(4,128)(2,1)} %copy.173), calls=%async_computation.7 | async-start | bytes 8388608 | tf_op jit(solution)/shard_map/all_to_all | solution.py:273
  1134.5 185.8 %all-reduce.22.cloned.1.call-start = ((), (), s32[]{:S(2)}) async-start(), calls=%async_computation.32 | async-start | bytes 155648
  1197.8 230.5 %reduce-scatter.21.cloned.1.call-start = ((), (), s32[]{:S(2)}) async-start(), calls=%async_computation.19 | async-start | bytes 2433024 | tf_op jit(solution)/shard_map/reduce_scatter | solution.py:306
  1201.8 329.8 %reduce-scatter.19.cloned.1.call-start = ((), (), s32[]{:S(2)}) async-start(), calls=%async_computation.18 | async-start | bytes 2433024 | tf_op jit(solution)/shard_map/reduce_scatter | solution.py:306
  1205.3 450.9 %reduce-scatter.17.cloned.1.call-start = ((), (), s32[]{:S(2)}) async-start(), calls=%async_computation.17 | async-start | bytes 7299072 | tf_op jit(solution)/shard_map/reduce_scatter | solution.py:304
  1212.6 567.6 %reduce-scatter.15.cloned.1.call-start = ((), (), s32[]{:S(2)}) async-start(), calls=%async_computation.16 | async-start | bytes 7299072 | tf_op jit(solution)/shard_map/reduce_scatter | solution.py:304
  1220.6 701.4 %reduce-scatter.25.cloned.1.call-start = ((), (), s32[]{:S(2)}) async-start(), calls=%async_computation.21 | async-start | bytes 9732096 | tf_op jit(solution)/shard_map/reduce_scatter | solution.py:308
  1230.2 832.1 %reduce-scatter.23.cloned.1.call-start = ((), (), s32[]{:S(2)}) async-start(), calls=%async_computation.20 | async-start | bytes 9732096 | tf_op jit(solution)/shard_map/reduce_scatter | solution.py:308
  1239.8 963.9 %reduce-scatter.29.cloned.1.call-start = ((), (), s32[]{:S(2)}) async-start(), calls=%async_computation.23 | async-start | bytes 9732096 | tf_op jit(solution)/shard_map/reduce_scatter | solution.py:310
  1250.9 1093.1 %reduce-scatter.27.cloned.1.call-start = ((), (), s32[]{:S(2)}) async-start(), calls=%async_computation.22 | async-start | bytes 9732096 | tf_op jit(solution)/shard_map/reduce_scatter | solution.py:310
  (186 other events, 813.4 us)
Sparse Core Ops, SparseCore 0:
  11.5 63.7 all-gather.28
  78.8 52.7 all-gather.30
  135.0 63.3 all-gather.32
  201.7 64.2 all-gather.34
  268.7 59.0 all-gather.36
  330.6 52.9 all-gather.38
  387.0 64.5 all-gather.40
  530.0 61.2 all-gather.42
  1197.9 122.2 all-reduce.21
  1326.2 102.0 reduce-scatter.20
  1433.6 97.9 reduce-scatter.18
  1538.1 118.0 reduce-scatter.16
  1661.8 118.3 reduce-scatter.14
  1787.0 134.9 reduce-scatter.24
  1927.8 134.5 reduce-scatter.22
  2069.1 134.5 reduce-scatter.28
  2209.4 134.5 reduce-scatter.26
where the time goes:
time: 2360 us; the launch traced here: 2350 us
  waiting for transfers between devices  1200 us (51%)
  matrix products  436 us (18%)
  blocking collectives  339 us (14%)
  other arithmetic  169 us (7%)
  local copies, waits for them, and re-layouts  153 us (6%)
  starting transfers between devices  29 us (1%)
    reduce_scatter x2, waiting for transfers between devices, body(): lax.psum_scatter(local_grads[6], ('dp', 'seq'), scatter_dimension=0, tile...  280 us
    reduce_scatter x2, waiting for transfers between devices, body(): lax.psum_scatter(local_grads[8], ('dp', 'seq'), scatter_dimension=0, tile...  280 us
    reduce_scatter x2, waiting for transfers between devices, body(): lax.psum_scatter(local_grads[2], ('dp', 'seq'), scatter_dimension=0, tile...  247 us
    reduce_scatter x2, waiting for transfers between devices, body(): lax.psum_scatter(local_grads[4], ('dp', 'seq'), scatter_dimension=0, tile...  203 us
    all_gather x2, blocking collectives, body(): lax.all_gather(shift_piece, ('dp', 'seq'), axis=1, tiled=True)  82.9 us
    all_gather x2, blocking collectives, body(): lax.all_gather(mixbias_piece, ('dp', 'seq'), axis=1, tiled=True)  82.6 us
    all_gather x2, blocking collectives, body(): lax.all_gather(gain_piece, ('dp', 'seq'), axis=1, tiled=True)  76.4 us
    dot_general x16, matrix products, block_scores(): jnp.einsum('qhd,khd->hqk', query_block, keys, preferred_element_type=jnp....  67.6 us
  transfers between devices with their start and end apart: 24, of which 15 were waited for; matrix products, arithmetic and copies ran while one was open for 16% of the time, Pallas kernels for 0%

commit v1 on v0

v1 whole, which is shorter than its diff:
```python
import functools

import jax
import jax.numpy as jnp
from jax import lax
from jax.experimental import pallas as pl
from jax.experimental.pallas import tpu as pltpu
from jax.sharding import PartitionSpec as P

D = 768
HD = 64
LAYERS = 2
SCALE = HD ** (-0.5)
norm_epsilon = 1e-05


def layer_norm(values, gain_row, shift_row):
    center = values - jnp.mean(values, axis=-1, keepdims=True)
    spread = jnp.mean(center * center, axis=-1, keepdims=True)
    return center * lax.rsqrt(spread + norm_epsilon) * gain_row + shift_row


def gelu_tanh(values):
    return jax.nn.gelu(values, approximate=True)


def product(spec, left, right):
    return jnp.einsum(spec, left, right, preferred_element_type=jnp.float32)


def dot_f32(left, right, left_dim, right_dim):
    return lax.dot_general(
        left, right, (((left_dim,), (right_dim,)), ((), ())), preferred_element_type=jnp.float32
    )


def causal(scores):
    key_place = lax.broadcasted_iota(jnp.int32, scores.shape, 0)
    query_place = lax.broadcasted_iota(jnp.int32, scores.shape, 1)
    return jnp.where(key_place <= query_place, scores, -1e30)


def score_block(qkv_ref, query, i, j):
    scores = dot_f32(qkv_ref[j, 1, 0], query, 0, 0)
    return causal(scores) if i == j else scores


def forward_kernel(qkv_ref, out_ref, log_ref):
    parts = qkv_ref.shape[0]
    for i in range(parts):
        query = qkv_ref[i, 0, 0] * jnp.asarray(SCALE, jnp.bfloat16)
        scores = [score_block(qkv_ref, query, i, j) for j in range(i + 1)]
        peak = functools.reduce(
            jnp.maximum, [jnp.max(block, axis=0, keepdims=True) for block in scores]
        )
        total = 0.0
        summed = 0.0
        for j in range(i + 1):
            weights = jnp.exp(scores[j] - peak)
            total = total + jnp.sum(weights, axis=0, keepdims=True)
            summed = summed + dot_f32(qkv_ref[j, 2, 0], weights.astype(jnp.bfloat16), 1, 0)
        out_ref[i, 0] = (summed / total).astype(jnp.bfloat16)
        log_ref[0, i] = peak + jnp.log(total)


def backward_kernel(qkv_ref, grad_ref, log_ref, out_ref, key_acc, value_acc):
    parts = qkv_ref.shape[0]
    for i in range(parts):
        query = qkv_ref[i, 0, 0] * jnp.asarray(SCALE, jnp.bfloat16)
        grad = grad_ref[i, 0]
        log_total = log_ref[0, i]
        shares = []
        share_grads = []
        inner = 0.0
        for j in range(i + 1):
            share = jnp.exp(score_block(qkv_ref, query, i, j) - log_total)
            share_grad = dot_f32(qkv_ref[j, 2, 0], grad, 0, 0)
            inner = inner + jnp.sum(share * share_grad, axis=0, keepdims=True)
            shares.append(share)
            share_grads.append(share_grad)
        query_grad = 0.0
        for j in range(i + 1):
            score_grad = (shares[j] * (share_grads[j] - inner)).astype(jnp.bfloat16)
            value_part = dot_f32(grad, shares[j].astype(jnp.bfloat16), 1, 1)
            key_part = dot_f32(query, score_grad, 1, 1)
            query_grad = query_grad + dot_f32(qkv_ref[j, 1, 0], score_grad, 1, 0)
            if i == j:
                key_acc[j] = key_part
                value_acc[j] = value_part
            else:
                key_acc[j] += key_part
                value_acc[j] += value_part
        out_ref[i, 0, 0] = (query_grad * SCALE).astype(jnp.bfloat16)
    for j in range(parts):
        out_ref[j, 1, 0] = key_acc[j].astype(jnp.bfloat16)
        out_ref[j, 2, 0] = value_acc[j].astype(jnp.bfloat16)


def attention_cost(qkv, products):
    parts, _, heads, width, length = qkv.shape
    pairs = parts * (parts + 1) // 2 * length * length * heads
    return pl.CostEstimate(
        flops=4 * products * pairs * width,
        transcendentals=pairs,
        bytes_accessed=2 * qkv.size * 2,
    )


def attend_forward(qkv):
    parts, _, heads, width, length = qkv.shape
    return pl.pallas_call(
        forward_kernel,
        grid=(heads,),
        in_specs=[pl.BlockSpec((parts, 3, 1, width, length), lambda h: (0, 0, h, 0, 0))],
        out_specs=[
            pl.BlockSpec((parts, 1, width, length), lambda h: (0, h, 0, 0)),
            pl.BlockSpec((1, parts, 1, length), lambda h: (h, 0, 0, 0)),
        ],
        out_shape=[
            jax.ShapeDtypeStruct((parts, heads, width, length), jnp.bfloat16),
            jax.ShapeDtypeStruct((heads, parts, 1, length), jnp.float32),
        ],
        compiler_params=pltpu.CompilerParams(vmem_limit_bytes=40 * 2**20),
        cost_estimate=attention_cost(qkv, 2),
    )(qkv)


def attend_backward(qkv, grad, log_total):
    parts, _, heads, width, length = qkv.shape
    qkv_spec = pl.BlockSpec((parts, 3, 1, width, length), lambda h: (0, 0, h, 0, 0))
    return pl.pallas_call(
        backward_kernel,
        grid=(heads,),
        in_specs=[
            qkv_spec,
            pl.BlockSpec((parts, 1, width, length), lambda h: (0, h, 0, 0)),
            pl.BlockSpec((1, parts, 1, length), lambda h: (h, 0, 0, 0)),
        ],
        out_specs=qkv_spec,
        out_shape=jax.ShapeDtypeStruct(qkv.shape, jnp.bfloat16),
        scratch_shapes=[
            pltpu.VMEM((parts, width, length), jnp.float32),
            pltpu.VMEM((parts, width, length), jnp.float32),
        ],
        compiler_params=pltpu.CompilerParams(vmem_limit_bytes=40 * 2**20),
        cost_estimate=attention_cost(qkv, 5),
    )(qkv, grad, log_total)


def place_bits():
    dp_bits = lax.axis_size("dp").bit_length() - 1
    seq_bits = lax.axis_size("seq").bit_length() - 1
    bits = [("dp", dp_bits - 1 - n) for n in range(dp_bits)]
    return bits + [("seq", seq_bits - 1 - n) for n in range(seq_bits)]


def my_bit(bit):
    return lax.rem(lax.axis_index(bit[0]) // (1 << bit[1]), 2)


def exchange(values, bit):
    name, place = bit
    count = lax.axis_size(name)
    return lax.ppermute(values, name, [(i, i ^ (1 << place)) for i in range(count)])


def sum_order(style):
    bits = place_bits()
    core, other, spread = bits[-1], bits[-2], bits[:-2][::-1]
    if style == 0:
        rest = [other] + spread
    elif style == 1:
        rest = spread + [other]
    else:
        rest = spread[1:2] + [other] + spread[:1] + spread[2:]
    return [core] + rest


def gather(piece, style):
    bits = place_bits()
    have = []
    block = piece
    for bit in reversed(sum_order(style)):
        axis = sum(1 for other in have if bits.index(other) < bits.index(bit))
        received = exchange(block, bit)
        shape = block.shape[:axis] + (2,) + block.shape[axis:]
        twice = jnp.broadcast_to(jnp.expand_dims(block, axis), shape)
        block = lax.dynamic_update_slice_in_dim(
            twice, jnp.expand_dims(received, axis), 1 - my_bit(bit), axis
        )
        have.append(bit)
    rows = piece.shape[0] * 2 ** len(bits)
    return block.reshape((rows,) + piece.shape[1:])


def scatter_sum(whole, style, sent=jnp.bfloat16):
    bits = place_bits()
    rows = whole.shape[0] >> len(bits)
    block = whole.reshape((2,) * len(bits) + (rows,) + whole.shape[1:])
    left = list(bits)
    for bit in sum_order(style):
        axis = left.index(bit)
        at = my_bit(bit)
        away = lax.dynamic_index_in_dim(block, 1 - at, axis, keepdims=False).astype(sent)
        kept = lax.dynamic_index_in_dim(block, at, axis, keepdims=False)
        block = kept + exchange(away, bit).astype(jnp.float32)
        left.remove(bit)
    return block


SMALL = (8, 128)


def body(
    tokens,
    cotangent,
    norm_gain,
    norm_shift,
    mixing_weight,
    mixing_bias,
    output_weight,
    output_bias,
    expand_weight,
    expand_bias,
    reduce_weight,
    reduce_bias,
):
    parts = lax.axis_size("seq")
    local_rows = tokens.shape[0]
    head_group = D // parts
    heads = head_group // HD

    small_members = (norm_gain, norm_shift, mixing_bias, output_bias, expand_bias, reduce_bias)
    flat = jnp.concatenate([member.reshape(-1) for member in small_members])
    slots = SMALL[0] * SMALL[1] * (-(-flat.shape[0] // (SMALL[0] * SMALL[1])))
    flat = jnp.pad(flat, (0, slots - flat.shape[0]))
    small = gather(flat.reshape(-1, 128), 0)
    small = small.reshape(-1, slots).astype(jnp.float32)
    devices = small.shape[0]
    small_rows = []
    start = 0
    for member in small_members:
        piece = small[:, start : start + member.size].reshape((devices,) + member.shape)
        start += member.size
        small_rows.append(jnp.moveaxis(piece, 0, -2).reshape(member.shape[:-1] + (-1,)))
    gains_all, shifts_all, mix_bias_all, out_bias_all, exp_bias_all, red_bias_all = small_rows

    def mixing_thirds(piece):
        return [gather(piece[:, n * D : (n + 1) * D], n) for n in range(3)]

    def later_weights(output_piece, expand_piece, reduce_piece):
        half = expand_piece.shape[1] // 2
        return (
            gather(output_piece, 2),
            (gather(expand_piece[:, :half], 0), gather(expand_piece[:, half:], 1)),
            gather(reduce_piece, 1),
        )

    mixing_first = mixing_thirds(mixing_weight[0])
    out_piece, exp_piece, red_piece, mixing_first = lax.optimization_barrier(
        (output_weight[0], expand_weight[0], reduce_weight[0], mixing_first)
    )
    first_rest = later_weights(out_piece, exp_piece, red_piece)
    mix_piece, out_piece, exp_piece, red_piece, first_rest = lax.optimization_barrier(
        (mixing_weight[1], output_weight[1], expand_weight[1], reduce_weight[1], first_rest)
    )
    mixing_second = mixing_thirds(mix_piece)
    second_rest = later_weights(out_piece, exp_piece, red_piece)
    weights = [(mixing_first,) + first_rest, (mixing_second,) + second_rest]

    hidden = tokens.astype(jnp.float32)
    saved = []
    for layer_index in range(LAYERS):
        mixing, output, expand, reduce = weights[layer_index]
        gains = gains_all[layer_index]
        shifts = shifts_all[layer_index]
        normed = layer_norm(hidden, gains[0], shifts[0]).astype(jnp.bfloat16)
        thirds = []
        for n in range(3):
            third = product("td,dc->ct", normed, mixing[n])
            if n != 1:
                third = third + mix_bias_all[layer_index, n // 2][:, None]
            thirds.append(third.astype(jnp.bfloat16).reshape(parts, heads, HD, local_rows))
        packed = lax.all_to_all(
            jnp.stack(thirds, axis=1), "seq", split_axis=0, concat_axis=0, tiled=True
        )
        attended, log_totals = attend_forward(packed)
        merged = lax.all_to_all(
            attended, "seq", split_axis=0, concat_axis=0, tiled=True
        ).reshape(D, local_rows)
        middle = hidden + (product("it,id->td", merged, output) + out_bias_all[layer_index])
        normed_two = layer_norm(middle, gains[1], shifts[1]).astype(jnp.bfloat16)
        pre_gelu = (
            jnp.concatenate([product("td,df->tf", normed_two, half) for half in expand], axis=1)
            + exp_bias_all[layer_index]
        )
        activated = gelu_tanh(pre_gelu).astype(jnp.bfloat16)
        saved.append((hidden, normed, packed, log_totals, merged, middle, normed_two, pre_gelu, activated))
        hidden = middle + (product("tf,fd->td", activated, reduce) + red_bias_all[layer_index])
    out_tokens = hidden.astype(jnp.bfloat16)

    running_grad = cotangent.astype(jnp.float32)
    large = [None] * LAYERS
    small_grads = [None] * LAYERS
    for layer_index in reversed(range(LAYERS)):
        layer_input, normed, packed, log_totals, merged, middle, normed_two, pre_gelu, activated = saved[
            layer_index
        ]
        mixing, output, expand, reduce = weights[layer_index]
        gains = gains_all[layer_index]
        shifts = shifts_all[layer_index]
        reduce_bias_grad = jnp.sum(running_grad, axis=0)
        grad_low = running_grad.astype(jnp.bfloat16)
        reduce_shard = scatter_sum(product("tf,td->fd", activated, grad_low), 1)
        act_grad = product("td,fd->tf", grad_low, reduce)
        unused_value, gelu_pull = jax.vjp(gelu_tanh, pre_gelu)
        pre_grad = gelu_pull(act_grad)[0].astype(jnp.bfloat16)
        expand_bias_grad = jnp.sum(pre_grad.astype(jnp.float32), axis=0)
        half = pre_grad.shape[1] // 2
        halves = (pre_grad[:, :half], pre_grad[:, half:])
        expand_shard = jnp.concatenate(
            [scatter_sum(product("td,tf->df", normed_two, halves[n]), 2 * n) for n in range(2)], axis=1
        )
        second_in = product("tf,df->td", halves[0], expand[0]) + product(
            "tf,df->td", halves[1], expand[1]
        )
        unused_norm, norm_pull = jax.vjp(layer_norm, middle, gains[1], shifts[1])
        middle_grad, gain_two, shift_two = norm_pull(second_in)
        running_grad = running_grad + middle_grad
        output_bias_grad = jnp.sum(running_grad, axis=0)
        out_low = running_grad.astype(jnp.bfloat16)
        output_shard = scatter_sum(product("it,td->id", merged, out_low), 2)
        merged_grad = product("td,id->it", out_low, output).astype(jnp.bfloat16)
        head_grad = lax.all_to_all(
            merged_grad.reshape(parts, heads, HD, local_rows),
            "seq",
            split_axis=0,
            concat_axis=0,
            tiled=True,
        )
        packed_grad = attend_backward(packed, head_grad, log_totals)
        mixed_grad = lax.all_to_all(
            packed_grad, "seq", split_axis=0, concat_axis=0, tiled=True
        )
        grad_thirds = [mixed_grad[:, n].reshape(D, local_rows) for n in range(3)]
        mixing_shard = jnp.concatenate(
            [scatter_sum(product("td,ct->dc", normed, grad_thirds[n]), n) for n in range(3)], axis=1
        )
        mixing_bias_grad = jnp.stack(
            [jnp.sum(grad_thirds[n].astype(jnp.float32), axis=1) for n in (0, 2)]
        )
        first_in = sum(product("ct,dc->td", grad_thirds[n], mixing[n]) for n in range(3))
        unused_first, first_pull = jax.vjp(layer_norm, layer_input, gains[0], shifts[0])
        input_part, gain_one, shift_one = first_pull(first_in)
        running_grad = running_grad + input_part
        large[layer_index] = (mixing_shard, output_shard, expand_shard, reduce_shard)
        small_grads[layer_index] = (
            jnp.stack([gain_one, gain_two]),
            jnp.stack([shift_one, shift_two]),
            mixing_bias_grad,
            output_bias_grad,
            expand_bias_grad,
            reduce_bias_grad,
        )

    rows = []
    for n, member in enumerate(small_members):
        both = jnp.stack([small_grads[index][n] for index in range(LAYERS)])
        both = both.reshape(both.shape[:-1] + (devices, -1))
        rows.append(jnp.moveaxis(both, -2, 0).reshape(devices, -1))
    packed_rows = jnp.concatenate(rows, axis=1)
    packed_rows = jnp.pad(packed_rows, ((0, 0), (0, slots - packed_rows.shape[1])))
    sums = scatter_sum(packed_rows.reshape(-1, 128), 0, jnp.float32).reshape(-1)
    shards = []
    start = 0
    for member in small_members:
        shards.append(sums[start : start + member.size].reshape(member.shape))
        start += member.size
    gain_out, shift_out, mix_bias_out, out_bias_out, exp_bias_out, red_bias_out = shards
    mixing_out, output_out, expand_out, reduce_out = (
        jnp.stack([large[index][n] for index in range(LAYERS)]) for n in range(4)
    )
    return (
        out_tokens,
        running_grad,
        gain_out,
        shift_out,
        mixing_out,
        mix_bias_out,
        output_out,
        out_bias_out,
        expand_out,
        exp_bias_out,
        reduce_out,
        red_bias_out,
    )


def solution(mesh):
    return jax.shard_map(
        body,
        mesh=mesh,
        in_specs=(
            P(("dp", "seq"), None),
            P(("dp", "seq"), None),
            P(None, None, ("dp", "seq")),
            P(None, None, ("dp", "seq")),
            P(None, ("dp", "seq"), None),
            P(None, None, ("dp", "seq")),
            P(None, ("dp", "seq"), None),
            P(None, ("dp", "seq")),
            P(None, ("dp", "seq"), None),
            P(None, ("dp", "seq")),
            P(None, ("dp", "seq"), None),
            P(None, ("dp", "seq")),
        ),
        out_specs=(
            P(("dp", "seq"), None),
            P(("dp", "seq"), None),
            P(None, None, ("dp", "seq")),
            P(None, None, ("dp", "seq")),
            P(None, ("dp", "seq"), None),
            P(None, None, ("dp", "seq")),
            P(None, ("dp", "seq"), None),
            P(None, ("dp", "seq")),
            P(None, ("dp", "seq"), None),
            P(None, ("dp", "seq")),
            P(None, ("dp", "seq"), None),
            P(None, ("dp", "seq")),
        ),
        check_vma=False,
    )
```

time: 2360 us -> 900 us (0.38)
  waiting for transfers between devices: 1200 us -> 341 us
  matrix products: 436 us -> 96.3 us
  blocking collectives: 339 us -> 0 us
  starting transfers between devices: 29 us -> 168 us
  other arithmetic: 169 us -> 52.3 us
  Pallas kernels: 0 us -> 75.9 us
    reduce_scatter x8 -> x0, waiting for transfers between devices: 1010 us -> none  [the longest x2 280 us: body(): lax.psum_scatter(local_grads[6], ('dp', 'seq'), scatter_dimension=0, tile...]
    dot_general x80 -> x42, matrix products: 436 us -> 96.3 us  [product(): return jnp.einsum(spec, left, right, preferred_element_type=jnp.float32)]
    ppermute x0 -> x150, waiting for transfers between devices: none -> 338 us  [exchange(): lax.ppermute(values, name, [(i, i ^ 1 << place) for i in range(count)])]
    all_gather x6 -> x0, blocking collectives: 242 us -> none  [the longest x2 82.9 us: body(): lax.all_gather(shift_piece, ('dp', 'seq'), axis=1, tiled=True)]
    ppermute x0 -> x150, starting transfers between devices: none -> 136 us  [exchange(): lax.ppermute(values, name, [(i, i ^ 1 << place) for i in range(count)])]
    all_to_all x7 -> x8, waiting for transfers between devices: 137 us -> 3 us  [the longest x2 2.98 us: body(): lax.all_to_all(attended, 'seq', split_axis=0, concat_axis=0, tiled=True)]
    pallas_call x0 -> x4, Pallas kernels: none -> 75.9 us  [the longest x2 49.7 us: attend_backward(): pl.pallas_call(backward_kernel, grid=(heads,), in_specs=[qkv_spec, pl.Blo...]
    convert_element_type x23 -> x3, other arithmetic: 59.2 us -> 1.81 us  [the longest x1 1.19 us: body(): normed = layer_norm(hidden, gains[0], shifts[0]).astype(jnp.bfloat16)]
  transfers between devices with their start and end apart: 24 -> 158, of which waited for: 15 -> 73; matrix products, arithmetic and copies ran while one was open for 16% -> 29% of each run, Pallas kernels for 0% -> 9%
where the time goes in v1:
time: 900 us; the launch traced here: 890 us
  waiting for transfers between devices  341 us (38%)
  starting transfers between devices  168 us (19%)
  local copies, waits for them, and re-layouts  151 us (17%)
  matrix products  96.3 us (11%)
  Pallas kernels  75.9 us (8%)
  other arithmetic  52.3 us (6%)
    ppermute x150, waiting for transfers between devices, exchange(): lax.ppermute(values, name, [(i, i ^ 1 << place) for i in range(count)])  338 us
    ppermute x150, starting transfers between devices, exchange(): lax.ppermute(values, name, [(i, i ^ 1 << place) for i in range(count)])  136 us
    dot_general x42, matrix products, product(): return jnp.einsum(spec, left, right, preferred_element_type=jnp.float32)  96.3 us
    pallas_call x2, Pallas kernels, attend_backward(): pl.pallas_call(backward_kernel, grid=(heads,), in_specs=[qkv_spec, pl.Blo...  49.7 us
    broadcast_in_dim x76, local copies, waits for them, and re-layouts, gather(): twice = jnp.broadcast_to(jnp.expand_dims(block, axis), shape)  37.2 us
    dynamic_update_slice x74, local copies, waits for them, and re-layouts, gather(): lax.dynamic_update_slice_in_dim(twice, jnp.expand_dims(received, axis), 1...  31.9 us
    add x70, other arithmetic, scatter_sum(): block = kept + exchange(away, bit).astype(jnp.float32)  31.4 us
    pallas_call x2, Pallas kernels, attend_forward(): pl.pallas_call(forward_kernel, grid=(heads,), in_specs=[pl.BlockSpec((par...  26.2 us
  transfers between devices with their start and end apart: 158, of which 73 were waited for; matrix products, arithmetic and copies ran while one was open for 29% of the time, Pallas kernels for 9%

profile of v1, /device:TPU:0, one launch (start us, length us, event | category | flops | bytes accessed | tf_op | source)
XLA Modules:
  0.0 890.3 jit_solution(7486644906969702035)
XLA Ops:
  5.4 4.1 collective-permute-start.15
  61.5 3.8 all-to-all-start
  74.2 24.3 %collective-permute-done.35 = bf16[96,768]{1,0:T(8,128)(2,1)S(1)} collective-permute-done((bf16[96,768]{1,0:T(8,128)(2,1)S(1)}, bf16[96,768]{1,0:T(8,128)(2,1)S(1)}, u32[]{:S(2)}, u32[]{:S(2)}) %collective-permute-start.35) | collective-permute-done | bytes 147488 | tf_op jit(solution)/shard_map/ppermute | solution.py:164
  102.2 15.6 %collective-permute-done.36 = bf16[2,96,768]{2,1,0:T(8,128)(2,1)S(1)} collective-permute-done((bf16[2,96,768]{2,1,0:T(8,128)(2,1)S(1)}, bf16[2,96,768]{2,1,0:T(8,128)(2,1)S(1)}, u32[]{:S(2)}, u32[]{:S(2)}) %collective-permute-start.36) | collective-permute-done | bytes 294944 | tf_op jit(solution)/shard_map/ppermute | solution.py:164
  121.4 12.7 %collective-permute-done.37 = bf16[2,2,96,768]{3,2,1,0:T(8,128)(2,1)S(1)} collective-permute-done((bf16[2,2,96,768]{3,2,1,0:T(8,128)(2,1)S(1)}, bf16[2,2,96,768]{3,2,1,0:T(8,128)(2,1)S(1)}, u32[]{:S(2)}, u32[]{:S(2)}) %collective-permute-start.37) | collective-permute-done | bytes 589856 | tf_op jit(solution)/shard_map/ppermute | solution.py:164
  136.5 3.9 collective-permute-done.32
  141.9 4.1 collective-permute-done.23
  147.6 15.6 %collective-permute-done.38 = bf16[2,2,2,96,768]{4,3,2,1,0:T(8,128)(2,1)S(1)} collective-permute-done((bf16[2,2,2,96,768]{4,3,2,1,0:T(8,128)(2,1)S(1)}, bf16[2,2,2,96,768]{4,3,2,1,0:T(8,128)(2,1)S(1)}, u32[]{:S(2)}, u32[]{:S(2)}) %collective-permute-start.38) | collective-permute-done | bytes 1179680 | tf_op jit(solution)/shard_map/ppermute | solution.py:164
  168.6 4.9 collective-permute-done.33
  184.1 12.6 %shard_map.211 = (bf16[4,3,64,512]{3,2,1,0:T(8,128)(2,1)}, f32[3,4,1,512]{3,2,1,0:T(1,128)S(1)}) custom-call(bf16[4,3,3,64,512]{4,3,2,1,0:T(8,128)(2,1)S(1)} %all-to-all-done.qkv_ref), custom_call_target="tpu_custom_call" | custom-call | flops 4026531840 | bytes 4718592 | tf_op jit(solution)/shard_map/pallas_call | solution.py:111
  196.7 4.5 all-to-all-start.1
  207.8 5.4 broadcast_in_dim.397
  225.2 6.8 fusion.173
  297.5 4.5 all-to-all-start.2
  317.3 15.5 %collective-permute-done.73 = bf16[2,2,2,96,768]{4,3,2,1,0:T(8,128)(2,1)S(1)} collective-permute-done((bf16[2,2,2,96,768]{4,3,2,1,0:T(8,128)(2,1)S(1)}, bf16[2,2,2,96,768]{4,3,2,1,0:T(8,128)(2,1)S(1)}, u32[]{:S(2)}, u32[]{:S(2)}) %collective-permute-start.73) | collective-permute-done | bytes 1179680 | tf_op jit(solution)/shard_map/ppermute | solution.py:164
  335.6 13.6 %shard_map.212 = (bf16[4,3,64,512]{3,2,1,0:T(8,128)(2,1)}, f32[3,4,1,512]{3,2,1,0:T(1,128)S(1)}) custom-call(bf16[4,3,3,64,512]{4,3,2,1,0:T(8,128)(2,1)} %all-to-all-done.2.qkv_ref), custom_call_target="tpu_custom_call" | custom-call | flops 4026531840 | bytes 4718592 | tf_op jit(solution)/shard_map/pallas_call | solution.py:111
  374.1 3.7 fusion.153
  379.9 4.0 broadcast_in_dim.865
  385.8 7.1 convert_reduce_fusion
  393.0 5.3 add_convert_fusion
  422.4 7.6 collective-permute-done.116
  440.5 25.1 %shard_map.213 = bf16[4,3,3,64,512]{4,3,2,1,0:T(8,128)(2,1)S(1)} custom-call(bf16[4,3,3,64,512]{4,3,2,1,0:T(8,128)(2,1)} %all-to-all-done.2.qkv_ref, bf16[4,3,64,512]{3,2,1,0:T(8,128)(2,1)S(1)} %all-to-all-done.4.grad_ref, f32[3,4,1,512]{3,2,1,0:T(1,128)S(1)} %get-tuple-element.46.log_ref), custom_call_target="tpu_custom_call" | custom-call | flops 10066329600 | bytes 4718592 | tf_op jit(solution)/shard_map/pallas_call | solution.py:131
  467.0 4.7 all-to-all-start.5
  486.4 4.2 collective-permute-done.136
  492.6 20.6 %collective-permute-done.131 = bf16[2,2,2,24,1536]{4,3,0,1,2:T(8,128)(2,1)S(1)} collective-permute-done((bf16[2,2,2,24,1536]{4,3,0,1,2:T(8,128)(2,1)S(1)}, bf16[2,2,2,24,1536]{4,3,0,1,2:T(8,128)(2,1)S(1)}, u32[]{:S(2)}, u32[]{:S(2)}) %collective-permute-start.131) | collective-permute-done | bytes 589856 | tf_op jit(solution)/shard_map/ppermute | solution.py:164
  514.7 4.4 collective-permute-done.137
  546.8 9.0 %convert_reduce_fusion.1 = (f32[3072]{0:T(1024)S(1)}, bf16[512,3072]{1,0:T(8,128)(2,1)S(1)}) fusion(f32[3072]{0:T(1024)S(1)} %copy-done.126, f32[512,1536]{1,0:T(8,128)S(1)} %copy-done.133, f32[512,1536]{1,0:T(8,128)S(1)} %copy-done.136, bf16[3072,768]{1,0:T(8,128)(2,1)} %bitcast.62, f32[512,768]{1,0:T(8,128)S(1)} %get-tuple-element.93), kind=kOutput, calls=%fused_computation.26 | convolution fusion | flops 2454057984 | bytes 15753216 | tf_op jit(solution)/shard_map/td,fd->tf/dot_general | solution.py:28
  570.9 3.7 all-to-all-start.6
  602.4 3.9 fusion.70
  613.1 24.6 %shard_map.214 = bf16[4,3,3,64,512]{4,3,2,1,0:T(8,128)(2,1)S(1)} custom-call(bf16[4,3,3,64,512]{4,3,2,1,0:T(8,128)(2,1)S(1)} %all-to-all-done.qkv_ref, bf16[4,3,64,512]{3,2,1,0:T(8,128)(2,1)S(1)} %all-to-all-done.6.grad_ref, f32[3,4,1,512]{3,2,1,0:T(1,128)S(1)} %get-tuple-element.47.log_ref), custom_call_target="tpu_custom_call" | custom-call | flops 10066329600 | bytes 4718592 | tf_op jit(solution)/shard_map/pallas_call | solution.py:131
  639.2 3.9 all-to-all-start.7
  651.7 11.4 %collective-permute-done.147 = bf16[2,2,96,768]{3,2,1,0:T(8,128)(2,1)S(1)} collective-permute-done((bf16[2,2,96,768]{3,2,1,0:T(8,128)(2,1)S(1)}, bf16[2,2,96,768]{3,2,1,0:T(8,128)(2,1)S(1)}, u32[]{:S(2)}, u32[]{:S(2)}) %collective-permute-start.147) | collective-permute-done | bytes 589856 | tf_op jit(solution)/shard_map/ppermute | solution.py:164
  664.3 4.8 collective-permute-done.106
  672.2 5.8 collective-permute-done.96
  680.4 12.6 %collective-permute-done.148 = bf16[2,96,768]{2,1,0:T(8,128)(2,1)S(1)} collective-permute-done((bf16[2,96,768]{2,1,0:T(8,128)(2,1)S(1)}, bf16[2,96,768]{2,1,0:T(8,128)(2,1)S(1)}, u32[]{:S(2)}, u32[]{:S(2)}) %collective-permute-start.148) | collective-permute-done | bytes 294944 | tf_op jit(solution)/shard_map/ppermute | solution.py:164
  694.3 4.4 collective-permute-done.102
  700.9 4.1 collective-permute-done.112
  709.5 6.0 collective-permute-done.103
  715.5 4.3 collective-permute-done.98
  724.2 5.0 collective-permute-done.109
  729.3 3.9 collective-permute-done.104
  733.2 5.1 collective-permute-done.99
  738.3 5.2 collective-permute-done.114
  748.5 11.4 %collective-permute-done.126 = bf16[2,2,2,24,1536]{4,3,0,1,2:T(8,128)(2,1)S(1)} collective-permute-done((bf16[2,2,2,24,1536]{4,3,0,1,2:T(8,128)(2,1)S(1)}, bf16[2,2,2,24,1536]{4,3,0,1,2:T(8,128)(2,1)S(1)}, u32[]{:S(2)}, u32[]{:S(2)}) %collective-permute-start.126) | collective-permute-done | bytes 589856 | tf_op jit(solution)/shard_map/ppermute | solution.py:164
  761.4 5.4 collective-permute-done.127
  826.3 17.3 %collective-permute-done.86 = bf16[2,2,2,24,768]{4,3,2,0,1:T(8,128)(2,1)S(1)} collective-permute-done((bf16[2,2,2,24,768]{4,3,2,0,1:T(8,128)(2,1)S(1)}, bf16[2,2,2,24,768]{4,3,2,0,1:T(8,128)(2,1)S(1)}, u32[]{:S(2)}, u32[]{:S(2)}) %collective-permute-start.86) | collective-permute-done | bytes 294944 | tf_op jit(solution)/shard_map/ppermute | solution.py:164
  862.0 10.9 %collective-permute-done.142 = bf16[2,2,96,768]{3,2,1,0:T(8,128)(2,1)S(1)} collective-permute-done((bf16[2,2,96,768]{3,2,1,0:T(8,128)(2,1)S(1)}, bf16[2,2,96,768]{3,2,1,0:T(8,128)(2,1)S(1)}, u32[]{:S(2)}, u32[]{:S(2)}) %collective-permute-start.142) | collective-permute-done | bytes 589856 | tf_op jit(solution)/shard_map/ppermute | solution.py:164
  875.0 8.9 collective-permute-done.143
  (1055 shorter events, 474.9 us)
Async XLA Ops:
  11.2 20.7 %collective-permute-start.5 = (bf16[24,768]{1,0:T(8,128)(2,1)S(1)}, bf16[24,768]{1,0:T(8,128)(2,1)S(1)}, u32[]{:S(2)}, u32[]{:S(2)}) collective-permute-start(bf16[24,768]{1,0:T(8,128)(2,1)S(1)} %get-tuple-element.121), channel_id=1, source_target_pairs={{0,2},{1,3},{2,0},{3,1},{4,6},{5,7},{6,4},{7,5},{8,10},{9,11},{10,... | collective-permute-start | bytes 110600 | tf_op jit(solution)/shard_map/ppermute | solution.py:164
  61.5 122.6 %all-to-all-start = ((bf16[4,3,3,64,512]{4,3,2,1,0:T(8,128)(2,1)}), bf16[4,3,3,64,512]{4,3,2,1,0:T(8,128)(2,1)S(1)}, u32[]{:S(2)}, u32[]{:S(2)}) async-start(bf16[4,3,3,64,512]{4,3,2,1,0:T(8,128)(2,1)} %pad_maximum_fusion), calls=%async_computation | async-start | bytes 4718592 | tf_op jit(solution)/shard_map/all_to_all | solution.py:284
  69.3 29.9 %collective-permute-start.30 = (bf16[24,1536]{1,0:T(8,128)(2,1)S(1)}, bf16[24,1536]{1,0:T(8,128)(2,1)S(1)}, u32[]{:S(2)}, u32[]{:S(2)}) collective-permute-start(bf16[24,1536]{1,0:T(8,128)(2,1)S(1)} %get-tuple-element.110), channel_id=1, source_target_pairs={{0,2},{1,3},{2,0},{3,1},{4,6},{5,7},{6,4},{7,5},{8,10},{9,11},{10,... | collective-permute-start | bytes 221192 | tf_op jit(solution)/shard_map/ppermute | solution.py:164
  71.3 27.2 %collective-permute-start.35 = (bf16[96,768]{1,0:T(8,128)(2,1)S(1)}, bf16[96,768]{1,0:T(8,128)(2,1)S(1)}, u32[]{:S(2)}, u32[]{:S(2)}) collective-permute-start(bf16[96,768]{1,0:T(8,128)(2,1)S(1)} %get-tuple-element.36), channel_id=1, source_target_pairs={{0,2},{1,3},{2,0},{3,1},{4,6},{5,7},{6,4},{7,5},{8,10},{9,11},{10,... | collective-permute-start | bytes 442376 | tf_op jit(solution)/shard_map/ppermute | solution.py:164
  71.4 30.3 %collective-permute-start.21 = (bf16[2,24,768]{2,1,0:T(8,128)(2,1)S(1)}, bf16[2,24,768]{2,1,0:T(8,128)(2,1)S(1)}, u32[]{:S(2)}, u32[]{:S(2)}) collective-permute-start(bf16[2,24,768]{2,1,0:T(8,128)(2,1)S(1)} %constant_dynamic-update-slice_fusion.4), channel_id=1, source_target_pairs={{0,4},{4,0},{8,12},{12,8},{16,20},{20,16},{24,28},{28,24},{1,5},{5... | collective-permute-start | bytes 221192 | tf_op jit(solution)/shard_map/ppermute | solution.py:164
  74.2 43.7 %collective-permute-start.26 = (bf16[2,24,1536]{2,1,0:T(8,128)(2,1)S(1)}, bf16[2,24,1536]{2,1,0:T(8,128)(2,1)S(1)}, u32[]{:S(2)}, u32[]{:S(2)}) collective-permute-start(bf16[2,24,1536]{2,1,0:T(8,128)(2,1)S(1)} %bitcast_dynamic-update-slice_fusion.57), channel_id=1, source_target_pairs={{0,8},{4,12},{8,0},{12,4},{16,24},{20,28},{24,16},{28,20},{1,9},{5... | collective-permute-start | bytes 442376 | tf_op jit(solution)/shard_map/ppermute | solution.py:164
  99.3 21.5 %collective-permute-start.31 = (bf16[2,24,1536]{2,1,0:T(8,128)(2,1)S(1)}, bf16[2,24,1536]{2,1,0:T(8,128)(2,1)S(1)}, u32[]{:S(2)}, u32[]{:S(2)}) collective-permute-start(bf16[2,24,1536]{2,1,0:T(8,128)(2,1)S(1)} %bitcast_dynamic-update-slice_fusion.56), channel_id=1, source_target_pairs={{0,16},{4,20},{8,24},{12,28},{16,0},{20,4},{24,8},{28,12},{1,17},{... | collective-permute-start | bytes 442376 | tf_op jit(solution)/shard_map/ppermute | solution.py:164
  101.7 33.9 %collective-permute-start.22 = (bf16[2,2,24,768]{3,2,1,0:T(8,128)(2,1)S(1)}, bf16[2,2,24,768]{3,2,1,0:T(8,128)(2,1)S(1)}, u32[]{:S(2)}, u32[]{:S(2)}) collective-permute-start(bf16[2,2,24,768]{3,2,1,0:T(8,128)(2,1)S(1)} %bitcast_dynamic-update-slice_fusion.58), channel_id=1, source_target_pairs={{0,2},{1,3},{2,0},{3,1},{4,6},{5,7},{6,4},{7,5},{8,10},{9,11},{10,... | collective-permute-start | bytes 442376 | tf_op jit(solution)/shard_map/ppermute | solution.py:164
  134.2 29.0 %collective-permute-start.38 = (bf16[2,2,2,96,768]{4,3,2,1,0:T(8,128)(2,1)S(1)}, bf16[2,2,2,96,768]{4,3,2,1,0:T(8,128)(2,1)S(1)}, u32[]{:S(2)}, u32[]{:S(2)}) collective-permute-start(bf16[2,2,2,96,768]{4,3,2,1,0:T(8,128)(2,1)S(1)} %bitcast_dynamic-update-slice_fusion.15), channel_id=1, source_target_pairs={{0,4},{4,0},{8,12},{12,8},{16,20},{20,16},{24,28},{28,24},{1,5},{5... | collective-permute-start | bytes 3538952 | tf_op jit(solution)/shard_map/ppermute | solution.py:164
  135.9 30.1 %collective-permute-start.28 = (bf16[2,2,2,24,1536]{4,3,2,1,0:T(8,128)(2,1)S(1)}, bf16[2,2,2,24,1536]{4,3,2,1,0:T(8,128)(2,1)S(1)}, u32[]{:S(2)}, u32[]{:S(2)}) collective-permute-start(bf16[2,2,2,24,1536]{4,3,2,1,0:T(8,128)(2,1)S(1)} %bitcast_dynamic-update-slice_fusion.31), channel_id=1, source_target_pairs={{0,2},{1,3},{2,0},{3,1},{4,6},{5,7},{6,4},{7,5},{8,10},{9,11},{10,... | collective-permute-start | bytes 1769480 | tf_op jit(solution)/shard_map/ppermute | solution.py:164
  140.5 33.0 %collective-permute-start.33 = (bf16[2,2,2,24,1536]{4,3,2,1,0:T(8,128)(2,1)S(1)}, bf16[2,2,2,24,1536]{4,3,2,1,0:T(8,128)(2,1)S(1)}, u32[]{:S(2)}, u32[]{:S(2)}) collective-permute-start(bf16[2,2,2,24,1536]{4,3,2,1,0:T(8,128)(2,1)S(1)} %bitcast_dynamic-update-slice_fusion.30), channel_id=1, source_target_pairs={{0,4},{4,0},{8,12},{12,8},{16,20},{20,16},{24,28},{28,24},{1,5},{5... | collective-permute-start | bytes 1769480 | tf_op jit(solution)/shard_map/ppermute | solution.py:164
  147.6 32.3 %collective-permute-start.24 = (bf16[2,2,2,2,24,768]{5,4,3,2,1,0:T(8,128)(2,1)}, bf16[2,2,2,2,24,768]{5,4,3,2,1,0:T(8,128)(2,1)}, u32[]{:S(2)}, u32[]{:S(2)}) collective-permute-start(bf16[2,2,2,2,24,768]{5,4,3,2,1,0:T(8,128)(2,1)} %bitcast_dynamic-update-slice_fusion.32), channel_id=1, source_target_pairs={{0,1},{1,0},{2,3},{3,2},{4,5},{5,4},{6,7},{7,6},{8,9},{9,8},{10,11... | collective-permute-start | bytes 1769480 | tf_op jit(solution)/shard_map/ppermute | solution.py:164
  165.9 41.9 %collective-permute-start.39 = (bf16[2,2,2,2,96,768]{5,4,3,2,1,0:T(8,128)(2,1)}, bf16[2,2,2,2,96,768]{5,4,3,2,1,0:T(8,128)(2,1)}, u32[]{:S(2)}, u32[]{:S(2)}) collective-permute-start(bf16[2,2,2,2,96,768]{5,4,3,2,1,0:T(8,128)(2,1)} %bitcast_dynamic-update-slice_fusion.5), channel_id=1, source_target_pairs={{0,1},{1,0},{2,3},{3,2},{4,5},{5,4},{6,7},{7,6},{8,9},{9,8},{10,11... | collective-permute-start | bytes 7077896 | tf_op jit(solution)/shard_map/ppermute | solution.py:164
  168.0 33.2 %collective-permute-start.29 = (bf16[2,2,2,2,24,1536]{5,4,3,2,1,0:T(8,128)(2,1)}, bf16[2,2,2,2,24,1536]{5,4,3,2,1,0:T(8,128)(2,1)}, u32[]{:S(2)}, u32[]{:S(2)}) collective-permute-start(bf16[2,2,2,2,24,1536]{5,4,3,2,1,0:T(8,128)(2,1)} %bitcast_dynamic-update-slice_fusion.17), channel_id=1, source_target_pairs={{0,1},{1,0},{2,3},{3,2},{4,5},{5,4},{6,7},{7,6},{8,9},{9,8},{10,11... | collective-permute-start | bytes 3538952 | tf_op jit(solution)/shard_map/ppermute | solution.py:164
  175.5 28.6 %collective-permute-start.34 = (bf16[2,2,2,2,24,1536]{5,4,3,2,1,0:T(8,128)(2,1)}, bf16[2,2,2,2,24,1536]{5,4,3,2,1,0:T(8,128)(2,1)}, u32[]{:S(2)}, u32[]{:S(2)}) collective-permute-start(bf16[2,2,2,2,24,1536]{5,4,3,2,1,0:T(8,128)(2,1)} %bitcast_dynamic-update-slice_fusion.16), channel_id=1, source_target_pairs={{0,1},{1,0},{2,3},{3,2},{4,5},{5,4},{6,7},{7,6},{8,9},{9,8},{10,11... | collective-permute-start | bytes 3538952 | tf_op jit(solution)/shard_map/ppermute | solution.py:164
  237.3 21.1 %collective-permute-start.70 = (bf16[96,768]{1,0:T(8,128)(2,1)S(1)}, bf16[96,768]{1,0:T(8,128)(2,1)}, u32[]{:S(2)}, u32[]{:S(2)}) collective-permute-start(bf16[96,768]{1,0:T(8,128)(2,1)S(1)} %get-tuple-element.45), channel_id=1, source_target_pairs={{0,2},{1,3},{2,0},{3,1},{4,6},{5,7},{6,4},{7,5},{8,10},{9,11},{10,... | collective-permute-start | bytes 442376 | tf_op jit(solution)/shard_map/ppermute | solution.py:164
  278.8 23.3 %collective-permute-start.58 = (bf16[2,2,2,24,768]{4,3,2,1,0:T(8,128)(2,1)S(1)}, bf16[2,2,2,24,768]{4,3,2,1,0:T(8,128)(2,1)}, u32[]{:S(2)}, u32[]{:S(2)}) collective-permute-start(bf16[2,2,2,24,768]{4,3,2,1,0:T(8,128)(2,1)S(1)} %bitcast_dynamic-update-slice_fusion.39), channel_id=1, source_target_pairs={{0,8},{4,12},{8,0},{12,4},{16,24},{20,28},{24,16},{28,20},{1,9},{5... | collective-permute-start | bytes 884744 | tf_op jit(solution)/shard_map/ppermute | solution.py:164
  297.5 38.0 %all-to-all-start.2 = ((bf16[4,3,3,64,512]{4,3,2,1,0:T(8,128)(2,1)}), bf16[4,3,3,64,512]{4,3,2,1,0:T(8,128)(2,1)}, u32[]{:S(2)}, u32[]{:S(2)}) async-start(bf16[4,3,3,64,512]{4,3,2,1,0:T(8,128)(2,1)} %pad_maximum_fusion.1), calls=%async_computation.2 | async-start | bytes 4718592 | tf_op jit(solution)/shard_map/all_to_all | solution.py:284
  304.8 28.0 %collective-permute-start.73 = (bf16[2,2,2,96,768]{4,3,2,1,0:T(8,128)(2,1)S(1)}, bf16[2,2,2,96,768]{4,3,2,1,0:T(8,128)(2,1)S(1)}, u32[]{:S(2)}, u32[]{:S(2)}) collective-permute-start(bf16[2,2,2,96,768]{4,3,2,1,0:T(8,128)(2,1)S(1)} %bitcast_dynamic-update-slice_fusion.8), channel_id=1, source_target_pairs={{0,4},{4,0},{8,12},{12,8},{16,20},{20,16},{24,28},{28,24},{1,5},{5... | collective-permute-start | bytes 3538952 | tf_op jit(solution)/shard_map/ppermute | solution.py:164
  310.6 42.3 %collective-permute-start.69 = (bf16[2,2,2,2,24,1536]{5,4,3,2,1,0:T(8,128)(2,1)}, bf16[2,2,2,2,24,1536]{5,4,3,2,1,0:T(8,128)(2,1)}, u32[]{:S(2)}, u32[]{:S(2)}) collective-permute-start(bf16[2,2,2,2,24,1536]{5,4,3,2,1,0:T(8,128)(2,1)} %bitcast_dynamic-update-slice_fusion.9), channel_id=1, source_target_pairs={{0,1},{1,0},{2,3},{3,2},{4,5},{5,4},{6,7},{7,6},{8,9},{9,8},{10,11... | collective-permute-start | bytes 3538952 | tf_op jit(solution)/shard_map/ppermute | solution.py:164
  314.8 41.0 %collective-permute-start.64 = (bf16[2,2,2,2,24,1536]{5,4,3,2,1,0:T(8,128)(2,1)}, bf16[2,2,2,2,24,1536]{5,4,3,2,1,0:T(8,128)(2,1)}, u32[]{:S(2)}, u32[]{:S(2)}) collective-permute-start(bf16[2,2,2,2,24,1536]{5,4,3,2,1,0:T(8,128)(2,1)} %bitcast_dynamic-update-slice_fusion.10), channel_id=1, source_target_pairs={{0,1},{1,0},{2,3},{3,2},{4,5},{5,4},{6,7},{7,6},{8,9},{9,8},{10,11... | collective-permute-start | bytes 3538952 | tf_op jit(solution)/shard_map/ppermute | solution.py:164
  335.6 44.3 %collective-permute-start.74 = (bf16[2,2,2,2,96,768]{5,4,3,2,1,0:T(8,128)(2,1)}, bf16[2,2,2,2,96,768]{5,4,3,2,1,0:T(8,128)(2,1)}, u32[]{:S(2)}, u32[]{:S(2)}) collective-permute-start(bf16[2,2,2,2,96,768]{5,4,3,2,1,0:T(8,128)(2,1)} %bitcast_dynamic-update-slice_fusion.2), channel_id=1, source_target_pairs={{0,1},{1,0},{2,3},{3,2},{4,5},{5,4},{6,7},{7,6},{8,9},{9,8},{10,11... | collective-permute-start | bytes 7077896 | tf_op jit(solution)/shard_map/ppermute | solution.py:164
  379.9 100.5 %collective-permute-start.145 = (bf16[2,2,2,2,96,768]{5,4,3,0,1,2:T(8,128)(2,1)}, bf16[2,2,2,2,96,768]{5,4,3,0,1,2:T(8,128)(2,1)}, u32[]{:S(2)}, u32[]{:S(2)}) collective-permute-start(bf16[2,2,2,2,96,768]{5,4,3,0,1,2:T(8,128)(2,1)} %fusion.22), channel_id=1, source_target_pairs={{0,1},{1,0},{2,3},{3,2},{4,5},{5,4},{6,7},{7,6},{8,9},{9,8},{10,11... | collective-permute-start | bytes 7077896 | tf_op jit(solution)/shard_map/ppermute | solution.py:164
  410.4 30.1 %all-to-all-start.4 = ((bf16[4,3,64,512]{3,2,1,0:T(8,128)(2,1)}), bf16[4,3,64,512]{3,2,1,0:T(8,128)(2,1)S(1)}, u32[]{:S(2)}, u32[]{:S(2)}) async-start(bf16[4,3,64,512]{3,2,1,0:T(8,128)(2,1)} %bitcast.761), calls=%async_computation.4 | async-start | bytes 1572864 | tf_op jit(solution)/shard_map/all_to_all | solution.py:334
  433.0 39.3 %collective-permute-start.135 = (bf16[2,2,2,2,24,1536]{5,4,0,2,3,1:T(8,128)(2,1)}, bf16[2,2,2,2,24,1536]{5,4,0,2,3,1:T(8,128)(2,1)}, u32[]{:S(2)}, u32[]{:S(2)}) collective-permute-start(bf16[2,2,2,2,24,1536]{5,4,0,2,3,1:T(8,128)(2,1)} %fusion.49), channel_id=1, source_target_pairs={{0,1},{1,0},{2,3},{3,2},{4,5},{5,4},{6,7},{7,6},{8,9},{9,8},{10,11... | collective-permute-start | bytes 3538952 | tf_op jit(solution)/shard_map/ppermute | solution.py:164
  437.7 38.9 %collective-permute-start.130 = (bf16[2,2,2,2,24,1536]{5,4,0,1,2,3:T(8,128)(2,1)}, bf16[2,2,2,2,24,1536]{5,4,0,1,2,3:T(8,128)(2,1)}, u32[]{:S(2)}, u32[]{:S(2)}) collective-permute-start(bf16[2,2,2,2,24,1536]{5,4,0,1,2,3:T(8,128)(2,1)} %fusion.48), channel_id=1, source_target_pairs={{0,1},{1,0},{2,3},{3,2},{4,5},{5,4},{6,7},{7,6},{8,9},{9,8},{10,11... | collective-permute-start | bytes 3538952 | tf_op jit(solution)/shard_map/ppermute | solution.py:164
  440.1 31.6 %collective-permute-start.119 = (bf16[24,768]{1,0:T(8,128)(2,1)S(1)}, bf16[24,768]{1,0:T(8,128)(2,1)S(1)}, u32[]{:S(2)}, u32[]{:S(2)}) collective-permute-start(bf16[24,768]{1,0:T(8,128)(2,1)S(1)} %fusion.129), channel_id=1, source_target_pairs={{0,16},{4,20},{8,24},{12,28},{16,0},{20,4},{24,8},{28,12},{1,17},{... | collective-permute-start | bytes 110600 | tf_op jit(solution)/shard_map/ppermute | solution.py:164
  467.0 68.2 %all-to-all-start.5 = ((bf16[4,3,3,64,512]{4,3,2,1,0:T(8,128)(2,1)}), bf16[4,3,3,64,512]{4,3,2,1,0:T(8,128)(2,1)}, u32[]{:S(2)}, u32[]{:S(2)}) async-start(bf16[4,3,3,64,512]{4,3,2,1,0:T(8,128)(2,1)} %copy-done.1), calls=%async_computation.5 | async-start | bytes 4718592 | tf_op jit(solution)/shard_map/all_to_all | solution.py:342
  478.3 34.9 %collective-permute-start.131 = (bf16[2,2,2,24,1536]{4,3,0,1,2:T(8,128)(2,1)S(1)}, bf16[2,2,2,24,1536]{4,3,0,1,2:T(8,128)(2,1)S(1)}, u32[]{:S(2)}, u32[]{:S(2)}) collective-permute-start(bf16[2,2,2,24,1536]{4,3,0,1,2:T(8,128)(2,1)S(1)} %fusion.58), channel_id=1, source_target_pairs={{0,2},{1,3},{2,0},{3,1},{4,6},{5,7},{6,4},{7,5},{8,10},{9,11},{10,... | collective-permute-start | bytes 1769480 | tf_op jit(solution)/shard_map/ppermute | solution.py:164
  485.3 123.0 %collective-permute-start.146 = (bf16[2,2,2,96,768]{4,3,2,0,1:T(8,128)(2,1)}, bf16[2,2,2,96,768]{4,3,2,0,1:T(8,128)(2,1)}, u32[]{:S(2)}, u32[]{:S(2)}) collective-permute-start(bf16[2,2,2,96,768]{4,3,2,0,1:T(8,128)(2,1)} %fusion.45), channel_id=1, source_target_pairs={{0,4},{4,0},{8,12},{12,8},{16,20},{20,16},{24,28},{28,24},{1,5},{5... | collective-permute-start | bytes 3538952 | tf_op jit(solution)/shard_map/ppermute | solution.py:164
  490.9 28.2 %collective-permute-start.137 = (bf16[2,2,24,1536]{3,2,0,1:T(8,128)(2,1)S(1)}, bf16[2,2,24,1536]{3,2,0,1:T(8,128)(2,1)S(1)}, u32[]{:S(2)}, u32[]{:S(2)}) collective-permute-start(bf16[2,2,24,1536]{3,2,0,1:T(8,128)(2,1)S(1)} %fusion.89), channel_id=1, source_target_pairs={{0,2},{1,3},{2,0},{3,1},{4,6},{5,7},{6,4},{7,5},{8,10},{9,11},{10,... | collective-permute-start | bytes 884744 | tf_op jit(solution)/shard_map/ppermute | solution.py:164
  570.9 42.2 %all-to-all-start.6 = ((bf16[4,3,64,512]{3,2,1,0:T(8,128)(2,1)}), bf16[4,3,64,512]{3,2,1,0:T(8,128)(2,1)S(1)}, u32[]{:S(2)}, u32[]{:S(2)}) async-start(bf16[4,3,64,512]{3,2,1,0:T(8,128)(2,1)} %bitcast.760), calls=%async_computation.6 | async-start | bytes 1572864 | tf_op jit(solution)/shard_map/all_to_all | solution.py:334
  585.7 57.4 %collective-permute-start.105 = (bf16[2,2,2,2,24,768]{5,4,0,2,3,1:T(8,128)(2,1)}, bf16[2,2,2,2,24,768]{5,4,0,2,3,1:T(8,128)(2,1)}, u32[]{:S(2)}, u32[]{:S(2)}) collective-permute-start(bf16[2,2,2,2,24,768]{5,4,0,2,3,1:T(8,128)(2,1)} %fusion.66), channel_id=1, source_target_pairs={{0,1},{1,0},{2,3},{3,2},{4,5},{5,4},{6,7},{7,6},{8,9},{9,8},{10,11... | collective-permute-start | bytes 1769480 | tf_op jit(solution)/shard_map/ppermute | solution.py:164
  588.2 57.2 %collective-permute-start.100 = (bf16[2,2,2,2,24,768]{5,4,3,0,1,2:T(8,128)(2,1)}, bf16[2,2,2,2,24,768]{5,4,3,0,1,2:T(8,128)(2,1)}, u32[]{:S(2)}, u32[]{:S(2)}) collective-permute-start(bf16[2,2,2,2,24,768]{5,4,3,0,1,2:T(8,128)(2,1)} %fusion.65), channel_id=1, source_target_pairs={{0,1},{1,0},{2,3},{3,2},{4,5},{5,4},{6,7},{7,6},{8,9},{9,8},{10,11... | collective-permute-start | bytes 1769480 | tf_op jit(solution)/shard_map/ppermute | solution.py:164
  590.9 56.1 %collective-permute-start.95 = (bf16[2,2,2,2,24,768]{5,4,0,1,2,3:T(8,128)(2,1)}, bf16[2,2,2,2,24,768]{5,4,0,1,2,3:T(8,128)(2,1)}, u32[]{:S(2)}, u32[]{:S(2)}) collective-permute-start(bf16[2,2,2,2,24,768]{5,4,0,1,2,3:T(8,128)(2,1)} %fusion.64), channel_id=1, source_target_pairs={{0,1},{1,0},{2,3},{3,2},{4,5},{5,4},{6,7},{7,6},{8,9},{9,8},{10,11... | collective-permute-start | bytes 1769480 | tf_op jit(solution)/shard_map/ppermute | solution.py:164
  595.9 53.1 %collective-permute-start.110 = (bf16[2,2,2,2,24,768]{5,4,3,2,1,0:T(8,128)(2,1)}, bf16[2,2,2,2,24,768]{5,4,3,2,1,0:T(8,128)(2,1)}, u32[]{:S(2)}, u32[]{:S(2)}) collective-permute-start(bf16[2,2,2,2,24,768]{5,4,3,2,1,0:T(8,128)(2,1)} %fusion.55), channel_id=1, source_target_pairs={{0,1},{1,0},{2,3},{3,2},{4,5},{5,4},{6,7},{7,6},{8,9},{9,8},{10,11... | collective-permute-start | bytes 1769480 | tf_op jit(solution)/shard_map/ppermute | solution.py:164
  608.3 137.4 %collective-permute-start.125 = (bf16[2,2,2,2,24,1536]{5,4,0,2,3,1:T(8,128)(2,1)}, bf16[2,2,2,2,24,1536]{5,4,0,2,3,1:T(8,128)(2,1)}, u32[]{:S(2)}, u32[]{:S(2)}) collective-permute-start(bf16[2,2,2,2,24,1536]{5,4,0,2,3,1:T(8,128)(2,1)} %fusion.47), channel_id=1, source_target_pairs={{0,1},{1,0},{2,3},{3,2},{4,5},{5,4},{6,7},{7,6},{8,9},{9,8},{10,11... | collective-permute-start | bytes 3538952 | tf_op jit(solution)/shard_map/ppermute | solution.py:164
  639.2 141.3 %all-to-all-start.7 = ((bf16[4,3,3,64,512]{4,3,2,1,0:T(8,128)(2,1)}), bf16[4,3,3,64,512]{4,3,2,1,0:T(8,128)(2,1)S(1)}, u32[]{:S(2)}, u32[]{:S(2)}) async-start(bf16[4,3,3,64,512]{4,3,2,1,0:T(8,128)(2,1)} %copy-done), calls=%async_computation.7 | async-start | bytes 4718592 | tf_op jit(solution)/shard_map/all_to_all | solution.py:342
  643.1 104.7 %collective-permute-start.120 = (bf16[2,2,2,2,24,1536]{5,4,0,1,2,3:T(8,128)(2,1)S(1)}, bf16[2,2,2,2,24,1536]{5,4,0,1,2,3:T(8,128)(2,1)S(1)}, u32[]{:S(2)}, u32[]{:S(2)}) collective-permute-start(bf16[2,2,2,2,24,1536]{5,4,0,1,2,3:T(8,128)(2,1)S(1)} %copy-done.67), channel_id=1, source_target_pairs={{0,1},{1,0},{2,3},{3,2},{4,5},{5,4},{6,7},{7,6},{8,9},{9,8},{10,11... | collective-permute-start | bytes 3538952 | tf_op jit(solution)/shard_map/ppermute | solution.py:164
  645.4 158.8 %collective-permute-start.140 = (bf16[2,2,2,2,96,768]{5,4,3,0,1,2:T(8,128)(2,1)}, bf16[2,2,2,2,96,768]{5,4,3,0,1,2:T(8,128)(2,1)}, u32[]{:S(2)}, u32[]{:S(2)}) collective-permute-start(bf16[2,2,2,2,96,768]{5,4,3,0,1,2:T(8,128)(2,1)} %fusion.21), channel_id=1, source_target_pairs={{0,1},{1,0},{2,3},{3,2},{4,5},{5,4},{6,7},{7,6},{8,9},{9,8},{10,11... | collective-permute-start | bytes 7077896 | tf_op jit(solution)/shard_map/ppermute | solution.py:164
  698.9 44.7 %collective-permute-start.149 = (bf16[96,768]{1,0:T(8,128)(2,1)S(1)}, bf16[96,768]{1,0:T(8,128)(2,1)S(1)}, u32[]{:S(2)}, u32[]{:S(2)}) collective-permute-start(bf16[96,768]{1,0:T(8,128)(2,1)S(1)} %fusion.107), channel_id=1, source_target_pairs={{0,2},{1,3},{2,0},{3,1},{4,6},{5,7},{6,4},{7,5},{8,10},{9,11},{10,... | collective-permute-start | bytes 442376 | tf_op jit(solution)/shard_map/ppermute | solution.py:164
  793.8 22.8 %collective-permute-start.90 = (bf16[2,2,2,2,24,768]{5,4,0,2,3,1:T(8,128)(2,1)}, bf16[2,2,2,2,24,768]{5,4,0,2,3,1:T(8,128)(2,1)}, u32[]{:S(2)}, u32[]{:S(2)}) collective-permute-start(bf16[2,2,2,2,24,768]{5,4,0,2,3,1:T(8,128)(2,1)} %fusion.63), channel_id=1, source_target_pairs={{0,1},{1,0},{2,3},{3,2},{4,5},{5,4},{6,7},{7,6},{8,9},{9,8},{10,11... | collective-permute-start | bytes 1769480 | tf_op jit(solution)/shard_map/ppermute | solution.py:164
  796.4 23.9 %collective-permute-start.85 = (bf16[2,2,2,2,24,768]{5,4,3,0,1,2:T(8,128)(2,1)}, bf16[2,2,2,2,24,768]{5,4,3,0,1,2:T(8,128)(2,1)}, u32[]{:S(2)}, u32[]{:S(2)}) collective-permute-start(bf16[2,2,2,2,24,768]{5,4,3,0,1,2:T(8,128)(2,1)} %fusion.62), channel_id=1, source_target_pairs={{0,1},{1,0},{2,3},{3,2},{4,5},{5,4},{6,7},{7,6},{8,9},{9,8},{10,11... | collective-permute-start | bytes 1769480 | tf_op jit(solution)/shard_map/ppermute | solution.py:164
  801.6 21.2 %collective-permute-start.80 = (bf16[2,2,2,2,24,768]{5,4,3,2,1,0:T(8,128)(2,1)S(1)}, bf16[2,2,2,2,24,768]{5,4,3,2,1,0:T(8,128)(2,1)}, u32[]{:S(2)}, u32[]{:S(2)}) collective-permute-start(bf16[2,2,2,2,24,768]{5,4,3,2,1,0:T(8,128)(2,1)S(1)} %fusion.54), channel_id=1, source_target_pairs={{0,1},{1,0},{2,3},{3,2},{4,5},{5,4},{6,7},{7,6},{8,9},{9,8},{10,11... | collective-permute-start | bytes 1769480 | tf_op jit(solution)/shard_map/ppermute | solution.py:164
  811.1 46.9 %collective-permute-start.141 = (bf16[2,2,2,96,768]{4,3,2,0,1:T(8,128)(2,1)}, bf16[2,2,2,96,768]{4,3,2,0,1:T(8,128)(2,1)}, u32[]{:S(2)}, u32[]{:S(2)}) collective-permute-start(bf16[2,2,2,96,768]{4,3,2,0,1:T(8,128)(2,1)} %fusion.44), channel_id=1, source_target_pairs={{0,4},{4,0},{8,12},{12,8},{16,20},{20,16},{24,28},{28,24},{1,5},{5... | collective-permute-start | bytes 3538952 | tf_op jit(solution)/shard_map/ppermute | solution.py:164
  821.7 21.9 %collective-permute-start.86 = (bf16[2,2,2,24,768]{4,3,2,0,1:T(8,128)(2,1)S(1)}, bf16[2,2,2,24,768]{4,3,2,0,1:T(8,128)(2,1)S(1)}, u32[]{:S(2)}, u32[]{:S(2)}) collective-permute-start(bf16[2,2,2,24,768]{4,3,2,0,1:T(8,128)(2,1)S(1)} %fusion.79), channel_id=1, source_target_pairs={{0,4},{4,0},{8,12},{12,8},{16,20},{20,16},{24,28},{28,24},{1,5},{5... | collective-permute-start | bytes 884744 | tf_op jit(solution)/shard_map/ppermute | solution.py:164
  824.1 21.5 %collective-permute-start.81 = (bf16[2,2,2,24,768]{4,3,2,1,0:T(8,128)(2,1)S(1)}, bf16[2,2,2,24,768]{4,3,2,1,0:T(8,128)(2,1)S(1)}, u32[]{:S(2)}, u32[]{:S(2)}) collective-permute-start(bf16[2,2,2,24,768]{4,3,2,1,0:T(8,128)(2,1)S(1)} %fusion.78), channel_id=1, source_target_pairs={{0,2},{1,3},{2,0},{3,1},{4,6},{5,7},{6,4},{7,5},{8,10},{9,11},{10,... | collective-permute-start | bytes 884744 | tf_op jit(solution)/shard_map/ppermute | solution.py:164
  825.1 21.6 %collective-permute-start.92 = (bf16[2,2,24,768]{3,2,0,1:T(8,128)(2,1)S(1)}, bf16[2,2,24,768]{3,2,0,1:T(8,128)(2,1)S(1)}, u32[]{:S(2)}, u32[]{:S(2)}) collective-permute-start(bf16[2,2,24,768]{3,2,0,1:T(8,128)(2,1)S(1)} %fusion.96), channel_id=1, source_target_pairs={{0,2},{1,3},{2,0},{3,1},{4,6},{5,7},{6,4},{7,5},{8,10},{9,11},{10,... | collective-permute-start | bytes 442376 | tf_op jit(solution)/shard_map/ppermute | solution.py:164
  (256 other events, 2036.5 us)

commit v2 on v1

--- a/solution.py
+++ b/solution.py
@@ -176,36 +176,71 @@
     return [core] + rest
 
 
-def gather(piece, style):
-    bits = place_bits()
-    have = []
-    block = piece
-    for bit in reversed(sum_order(style)):
-        axis = sum(1 for other in have if bits.index(other) < bits.index(bit))
-        received = exchange(block, bit)
-        shape = block.shape[:axis] + (2,) + block.shape[axis:]
-        twice = jnp.broadcast_to(jnp.expand_dims(block, axis), shape)
-        block = lax.dynamic_update_slice_in_dim(
+class Gather:
+    def __init__(self, piece, style):
+        self.bits = place_bits()
+        self.order = list(reversed(sum_order(style)))
+        self.have = []
+        self.block = piece
+        self.tail = (piece.shape[0] << len(self.bits),) + piece.shape[1:]
+
+    def step(self):
+        if len(self.have) == len(self.order):
+            return
+        bit = self.order[len(self.have)]
+        axis = sum(1 for other in self.have if self.bits.index(other) < self.bits.index(bit))
+        received = exchange(self.block, bit)
+        shape = self.block.shape[:axis] + (2,) + self.block.shape[axis:]
+        twice = jnp.broadcast_to(jnp.expand_dims(self.block, axis), shape)
+        self.block = lax.dynamic_update_slice_in_dim(
             twice, jnp.expand_dims(received, axis), 1 - my_bit(bit), axis
         )
-        have.append(bit)
-    rows = piece.shape[0] * 2 ** len(bits)
-    return block.reshape((rows,) + piece.shape[1:])
-
-
-def scatter_sum(whole, style, sent=jnp.bfloat16):
-    bits = place_bits()
-    rows = whole.shape[0] >> len(bits)
-    block = whole.reshape((2,) * len(bits) + (rows,) + whole.shape[1:])
-    left = list(bits)
-    for bit in sum_order(style):
-        axis = left.index(bit)
+        self.have.append(bit)
+
+    def result(self):
+        return self.block.reshape(self.tail)
+
+
+class ScatterSum:
+    def __init__(self, whole, style, sent=jnp.bfloat16):
+        bits = place_bits()
+        rows = whole.shape[0] >> len(bits)
+        self.block = whole.reshape((2,) * len(bits) + (rows,) + whole.shape[1:])
+        self.left = list(bits)
+        self.order = sum_order(style)
+        self.sent = sent
+
+    def step(self):
+        if not self.left:
+            return
+        bit = self.order[-len(self.left)]
+        axis = self.left.index(bit)
         at = my_bit(bit)
-        away = lax.dynamic_index_in_dim(block, 1 - at, axis, keepdims=False).astype(sent)
-        kept = lax.dynamic_index_in_dim(block, at, axis, keepdims=False)
-        block = kept + exchange(away, bit).astype(jnp.float32)
-        left.remove(bit)
-    return block
+        away = lax.dynamic_index_in_dim(self.block, 1 - at, axis, keepdims=False)
+        kept = lax.dynamic_index_in_dim(self.block, at, axis, keepdims=False)
+        self.block = kept + exchange(away.astype(self.sent), bit).astype(jnp.float32)
+        self.left.remove(bit)
+
+    def result(self):
+        return self.block
+
+
+def advance(movers, steps):
+    for _ in range(steps):
+        for mover in movers:
+            mover.step()
+
+
+def finish(movers):
+    advance(movers, len(place_bits()))
+    return [mover.result() for mover in movers]
+
+
+def hold(value, movers):
+    value, blocks = lax.optimization_barrier((value, [mover.block for mover in movers]))
+    for mover, block in zip(movers, blocks):
+        mover.block = block
+    return value
 
 
 SMALL = (8, 128)
@@ -230,11 +265,31 @@
     head_group = D // parts
     heads = head_group // HD
 
+    def mixing_gathers(piece, cuts):
+        width = piece.shape[1] // cuts
+        return [Gather(piece[:, n * width : (n + 1) * width], n) for n in range(cuts)]
+
+    def later_weights(output_piece, expand_piece, reduce_piece):
+        rows = output_piece.shape[0]
+        flat = jnp.concatenate([output_piece, expand_piece, reduce_piece.reshape(rows, -1)], axis=1)
+        width = flat.shape[1] // 3
+        return [Gather(flat[:, n * width : (n + 1) * width], n) for n in range(3)]
+
+    def split_weights(chunks):
+        half = expand_weight.shape[2] // 2
+        first, second, third = chunks
+        expand = (first[:, D:], second[:, :half])
+        reduce = jnp.concatenate([second[:, half:], third], axis=1).reshape(-1, D)
+        return first[:, :D], expand, reduce
+
     small_members = (norm_gain, norm_shift, mixing_bias, output_bias, expand_bias, reduce_bias)
     flat = jnp.concatenate([member.reshape(-1) for member in small_members])
     slots = SMALL[0] * SMALL[1] * (-(-flat.shape[0] // (SMALL[0] * SMALL[1])))
     flat = jnp.pad(flat, (0, slots - flat.shape[0]))
-    small = gather(flat.reshape(-1, 128), 0)
+    small_mover = Gather(flat.reshape(-1, 128), 0)
+    mixing_movers = mixing_gathers(mixing_weight[0], 3)
+    rest_movers = later_weights(output_weight[0], expand_weight[0], reduce_weight[0])
+    small = finish([small_mover] + mixing_movers)[0]
     small = small.reshape(-1, slots).astype(jnp.float32)
     devices = small.shape[0]
     small_rows = []
@@ -245,35 +300,17 @@
         small_rows.append(jnp.moveaxis(piece, 0, -2).reshape(member.shape[:-1] + (-1,)))
     gains_all, shifts_all, mix_bias_all, out_bias_all, exp_bias_all, red_bias_all = small_rows
 
-    def mixing_thirds(piece):
-        return [gather(piece[:, n * D : (n + 1) * D], n) for n in range(3)]
-
-    def later_weights(output_piece, expand_piece, reduce_piece):
-        half = expand_piece.shape[1] // 2
-        return (
-            gather(output_piece, 2),
-            (gather(expand_piece[:, :half], 0), gather(expand_piece[:, half:], 1)),
-            gather(reduce_piece, 1),
-        )
-
-    mixing_first = mixing_thirds(mixing_weight[0])
-    out_piece, exp_piece, red_piece, mixing_first = lax.optimization_barrier(
-        (output_weight[0], expand_weight[0], reduce_weight[0], mixing_first)
-    )
-    first_rest = later_weights(out_piece, exp_piece, red_piece)
-    mix_piece, out_piece, exp_piece, red_piece, first_rest = lax.optimization_barrier(
-        (mixing_weight[1], output_weight[1], expand_weight[1], reduce_weight[1], first_rest)
-    )
-    mixing_second = mixing_thirds(mix_piece)
-    second_rest = later_weights(out_piece, exp_piece, red_piece)
-    weights = [(mixing_first,) + first_rest, (mixing_second,) + second_rest]
-
     hidden = tokens.astype(jnp.float32)
     saved = []
+    weights = []
     for layer_index in range(LAYERS):
-        mixing, output, expand, reduce = weights[layer_index]
+        mixing = finish(mixing_movers)
+        if len(mixing) == 1:
+            mixing = [mixing[0][:, n * D : (n + 1) * D] for n in range(3)]
         gains = gains_all[layer_index]
         shifts = shifts_all[layer_index]
+        mixing = hold(mixing, rest_movers)
+        advance(rest_movers, 2)
         normed = layer_norm(hidden, gains[0], shifts[0]).astype(jnp.bfloat16)
         thirds = []
         for n in range(3):
@@ -284,10 +321,23 @@
         packed = lax.all_to_all(
             jnp.stack(thirds, axis=1), "seq", split_axis=0, concat_axis=0, tiled=True
         )
+        advance(rest_movers, 2)
         attended, log_totals = attend_forward(packed)
+        advance(rest_movers, 1)
         merged = lax.all_to_all(
             attended, "seq", split_axis=0, concat_axis=0, tiled=True
         ).reshape(D, local_rows)
+        output, expand, reduce = split_weights(finish(rest_movers))
+        weights.append((mixing, output, expand, reduce))
+        if layer_index + 1 < LAYERS:
+            following = layer_index + 1
+            mixing_movers = mixing_gathers(mixing_weight[following], 1)
+            rest_movers = later_weights(
+                output_weight[following], expand_weight[following], reduce_weight[following]
+            )
+            merged = hold(merged, mixing_movers + rest_movers)
+            advance(mixing_movers, 5)
+            advance(rest_movers, 1)
         middle = hidden + (product("it,id->td", merged, output) + out_bias_all[layer_index])
         normed_two = layer_norm(middle, gains[1], shifts[1]).astype(jnp.bfloat16)
         pre_gelu = (
@@ -302,6 +352,7 @@
     running_grad = cotangent.astype(jnp.float32)
     large = [None] * LAYERS
     small_grads = [None] * LAYERS
+    previous = []
     for layer_index in reversed(range(LAYERS)):
         layer_input, normed, packed, log_totals, merged, middle, normed_two, pre_gelu, activated = saved[
             layer_index
@@ -311,16 +362,18 @@
         shifts = shifts_all[layer_index]
         reduce_bias_grad = jnp.sum(running_grad, axis=0)
         grad_low = running_grad.astype(jnp.bfloat16)
-        reduce_shard = scatter_sum(product("tf,td->fd", activated, grad_low), 1)
+        reduce_mover = ScatterSum(product("tf,td->fd", activated, grad_low), 1)
+        reduce_mover.step()
         act_grad = product("td,fd->tf", grad_low, reduce)
         unused_value, gelu_pull = jax.vjp(gelu_tanh, pre_gelu)
         pre_grad = gelu_pull(act_grad)[0].astype(jnp.bfloat16)
         expand_bias_grad = jnp.sum(pre_grad.astype(jnp.float32), axis=0)
+        advance(previous, 1)
+        reduce_mover.step()
+        expand_movers = [ScatterSum(product("td,tf->df", normed_two, pre_grad), 2)]
+        advance(expand_movers, 1)
         half = pre_grad.shape[1] // 2
         halves = (pre_grad[:, :half], pre_grad[:, half:])
-        expand_shard = jnp.concatenate(
-            [scatter_sum(product("td,tf->df", normed_two, halves[n]), 2 * n) for n in range(2)], axis=1
-        )
         second_in = product("tf,df->td", halves[0], expand[0]) + product(
             "tf,df->td", halves[1], expand[1]
         )
@@ -329,7 +382,10 @@
         running_grad = running_grad + middle_grad
         output_bias_grad = jnp.sum(running_grad, axis=0)
         out_low = running_grad.astype(jnp.bfloat16)
-        output_shard = scatter_sum(product("it,td->id", merged, out_low), 2)
+        finish(previous)
+        output_mover = ScatterSum(product("it,td->id", merged, out_low), 0)
+        output_mover.step()
+        movers = [reduce_mover] + expand_movers + [output_mover]
         merged_grad = product("td,id->it", out_low, output).astype(jnp.bfloat16)
         head_grad = lax.all_to_all(
             merged_grad.reshape(parts, heads, HD, local_rows),
@@ -338,14 +394,21 @@
             concat_axis=0,
             tiled=True,
         )
+        advance(movers, 2)
         packed_grad = attend_backward(packed, head_grad, log_totals)
+        advance(movers, 1)
         mixed_grad = lax.all_to_all(
             packed_grad, "seq", split_axis=0, concat_axis=0, tiled=True
         )
         grad_thirds = [mixed_grad[:, n].reshape(D, local_rows) for n in range(3)]
-        mixing_shard = jnp.concatenate(
-            [scatter_sum(product("td,ct->dc", normed, grad_thirds[n]), n) for n in range(3)], axis=1
-        )
+        if layer_index:
+            all_thirds = jnp.concatenate(grad_thirds, axis=0)
+            mixing_movers = [ScatterSum(product("td,ct->dc", normed, all_thirds), 0)]
+        else:
+            mixing_movers = [
+                ScatterSum(product("td,ct->dc", normed, grad_thirds[n]), n) for n in range(3)
+            ]
+        advance(mixing_movers, 2)
         mixing_bias_grad = jnp.stack(
             [jnp.sum(grad_thirds[n].astype(jnp.float32), axis=1) for n in (0, 2)]
         )
@@ -353,7 +416,9 @@
         unused_first, first_pull = jax.vjp(layer_norm, layer_input, gains[0], shifts[0])
         input_part, gain_one, shift_one = first_pull(first_in)
         running_grad = running_grad + input_part
-        large[layer_index] = (mixing_shard, output_shard, expand_shard, reduce_shard)
+        finish(movers)
+        previous = mixing_movers
+        large[layer_index] = (mixing_movers, [output_mover], expand_movers, [reduce_mover])
         small_grads[layer_index] = (
             jnp.stack([gain_one, gain_two]),
             jnp.stack([shift_one, shift_two]),
@@ -370,7 +435,8 @@
         rows.append(jnp.moveaxis(both, -2, 0).reshape(devices, -1))
     packed_rows = jnp.concatenate(rows, axis=1)
     packed_rows = jnp.pad(packed_rows, ((0, 0), (0, slots - packed_rows.shape[1])))
-    sums = scatter_sum(packed_rows.reshape(-1, 128), 0, jnp.float32).reshape(-1)
+    small_sum = ScatterSum(packed_rows.reshape(-1, 128), 0, jnp.float32)
+    sums = finish(previous + [small_sum])[-1].reshape(-1)
     shards = []
     start = 0
     for member in small_members:
@@ -378,7 +444,13 @@
         start += member.size
     gain_out, shift_out, mix_bias_out, out_bias_out, exp_bias_out, red_bias_out = shards
     mixing_out, output_out, expand_out, reduce_out = (
-        jnp.stack([large[index][n] for index in range(LAYERS)]) for n in range(4)
+        jnp.stack(
+            [
+                jnp.concatenate([mover.result() for mover in large[index][n]], axis=1)
+                for index in range(LAYERS)
+            ]
+        )
+        for n in range(4)
     )
     return (
         out_tokens,

time: 900 us -> 822 us (0.913)
  waiting for transfers between devices: 341 us -> 264 us
  starting transfers between devices: 168 us -> 141 us
  matrix products: 96.3 us -> 112 us
  other arithmetic: 52.3 us -> 62.9 us
    ppermute x150 -> x110, waiting for transfers between devices: 338 us -> 238 us  [exchange(): lax.ppermute(values, name, [(i, i ^ 1 << place) for i in range(count)])]
    ppermute x150 -> x110, starting transfers between devices: 136 us -> 108 us  [exchange(): lax.ppermute(values, name, [(i, i ^ 1 << place) for i in range(count)])]
    reshape x0 -> x2, local copies, waits for them, and re-layouts: none -> 17.1 us  [split_weights(): reduce = jnp.concatenate([second[:, half:], third], axis=1).reshape(-1, D)]
    broadcast_in_dim x76 -> x56, local copies, waits for them, and re-layouts: 37.2 us -> 21.6 us  [step(): twice = jnp.broadcast_to(jnp.expand_dims(self.block, axis), shape)]
    dot_general x42 -> x38, matrix products: 96.3 us -> 112 us  [product(): return jnp.einsum(spec, left, right, preferred_element_type=jnp.float32)]
    dynamic_update_slice x74 -> x53, local copies, waits for them, and re-layouts: 31.9 us -> 20.2 us  [step(): lax.dynamic_update_slice_in_dim(twice, jnp.expand_dims(received, axis), 1...]
    all_to_all x2, waiting for transfers between devices: 2.98 us -> 13.3 us  [body(): lax.all_to_all(attended, 'seq', split_axis=0, concat_axis=0, tiled=True)]
    convert_element_type x70 -> x50, local copies, waits for them, and re-layouts: 23.5 us -> 28.4 us  [step(): away.astype(self.sent)]
  transfers between devices with their start and end apart: 158 -> 118, of which waited for: 73 -> 48; matrix products, arithmetic and copies ran while one was open for 29% -> 33% of each run, Pallas kernels for 9% -> 9%
where the time goes in v2:
time: 822 us; the launch traced here: 812 us
  waiting for transfers between devices  264 us (32%)
  local copies, waits for them, and re-layouts  152 us (18%)
  starting transfers between devices  141 us (17%)
  matrix products  112 us (14%)
  Pallas kernels  75.9 us (9%)
  other arithmetic  62.9 us (8%)
    ppermute x110, waiting for transfers between devices, exchange(): lax.ppermute(values, name, [(i, i ^ 1 << place) for i in range(count)])  238 us
    dot_general x38, matrix products, product(): return jnp.einsum(spec, left, right, preferred_element_type=jnp.float32)  112 us
    ppermute x110, starting transfers between devices, exchange(): lax.ppermute(values, name, [(i, i ^ 1 << place) for i in range(count)])  108 us
    pallas_call x2, Pallas kernels, attend_backward(): pl.pallas_call(backward_kernel, grid=(heads,), in_specs=[qkv_spec, pl.Blo...  49.7 us
    add x47, other arithmetic, step(): kept + exchange(away.astype(self.sent), bit).astype(jnp.float32)  34.2 us
    convert_element_type x50, local copies, waits for them, and re-layouts, step(): away.astype(self.sent)  28.4 us
    pallas_call x2, Pallas kernels, attend_forward(): pl.pallas_call(forward_kernel, grid=(heads,), in_specs=[pl.BlockSpec((par...  26.2 us
    unnamed x283, local copies, waits for them, and re-layouts  24.7 us
  transfers between devices with their start and end apart: 118, of which 48 were waited for; matrix products, arithmetic and copies ran while one was open for 33% of the time, Pallas kernels for 9%

profile of v2, /device:TPU:0, one launch (start us, length us, event | category | flops | bytes accessed | tf_op | source)
XLA Modules:
  0.0 811.7 jit_solution(1309216314174669669)
XLA Ops:
  5.2 4.1 collective-permute-start.15
  43.2 3.9 collective-permute-done.12
  49.8 5.1 collective-permute-done.13
  67.7 4.1 all-to-all-start
  82.6 4.8 collective-permute-done.21
  94.1 15.6 %collective-permute-done.32 = bf16[2,2,24,2304]{3,2,1,0:T(8,128)(2,1)S(1)} collective-permute-done((bf16[2,2,24,2304]{3,2,1,0:T(8,128)(2,1)S(1)}, bf16[2,2,24,2304]{3,2,1,0:T(8,128)(2,1)S(1)}, u32[]{:S(2)}, u32[]{:S(2)}) %collective-permute-start.32) | collective-permute-done | bytes 442400 | tf_op jit(solution)/shard_map/ppermute | solution.py:164
  114.7 12.6 %shard_map.211 = (bf16[4,3,64,512]{3,2,1,0:T(8,128)(2,1)}, f32[3,4,1,512]{3,2,1,0:T(1,128)S(1)}) custom-call(bf16[4,3,3,64,512]{4,3,2,1,0:T(8,128)(2,1)S(1)} %all-to-all-done.qkv_ref), custom_call_target="tpu_custom_call" | custom-call | flops 4026531840 | bytes 4718592 | tf_op jit(solution)/shard_map/pallas_call | solution.py:111
  127.4 4.2 all-to-all-start.1
  136.1 7.9 all-to-all-done.1
  152.0 5.7 collective-permute-done.28
  166.6 6.4 collective-permute-done.37
  181.3 15.4 %collective-permute-done.38 = bf16[2,2,2,24,2304]{4,3,2,1,0:T(8,128)(2,1)S(1)} collective-permute-done((bf16[2,2,2,24,2304]{4,3,2,1,0:T(8,128)(2,1)S(1)}, bf16[2,2,2,24,2304]{4,3,2,1,0:T(8,128)(2,1)S(1)}, u32[]{:S(2)}, u32[]{:S(2)}) %collective-permute-start.38) | collective-permute-done | bytes 884768 | tf_op jit(solution)/shard_map/ppermute | solution.py:164
  208.4 8.8 %collective-permute-done.47 = bf16[2,24,2304]{2,1,0:T(8,128)(2,1)S(1)} collective-permute-done((bf16[2,24,2304]{2,1,0:T(8,128)(2,1)S(1)}, bf16[2,24,2304]{2,1,0:T(8,128)(2,1)S(1)}, u32[]{:S(2)}, u32[]{:S(2)}) %collective-permute-start.47) | collective-permute-done | bytes 221216 | tf_op jit(solution)/shard_map/ppermute | solution.py:164
  219.2 9.8 %collective-permute-done.48 = bf16[2,2,24,2304]{3,2,1,0:T(8,128)(2,1)S(1)} collective-permute-done((bf16[2,2,24,2304]{3,2,1,0:T(8,128)(2,1)S(1)}, bf16[2,2,24,2304]{3,2,1,0:T(8,128)(2,1)S(1)}, u32[]{:S(2)}, u32[]{:S(2)}) %collective-permute-start.48) | collective-permute-done | bytes 442400 | tf_op jit(solution)/shard_map/ppermute | solution.py:164
  231.9 19.9 %collective-permute-done.49 = bf16[2,2,2,24,2304]{4,3,2,1,0:T(8,128)(2,1)S(1)} collective-permute-done((bf16[2,2,2,24,2304]{4,3,2,1,0:T(8,128)(2,1)S(1)}, bf16[2,2,2,24,2304]{4,3,2,1,0:T(8,128)(2,1)S(1)}, u32[]{:S(2)}, u32[]{:S(2)}) %collective-permute-start.49) | collective-permute-done | bytes 884768 | tf_op jit(solution)/shard_map/ppermute | solution.py:164
  270.6 8.7 %reshape.539 = bf16[3072,768]{1,0:T(8,128)(2,1)} reshape(bf16[768,3072]{1,0:T(8,128)(2,1)} %pad_maximum_fusion) | data formatting | bytes 9437184 | tf_op jit(solution)/shard_map/reshape | solution.py:282
  279.3 8.7 %fusion.183 = (f32[512]{0:T(512)S(1)}, f32[512,768]{1,0:T(8,128)S(1)}) fusion(f32[512,768]{1,0:T(8,128)} %copy-done.24, f32[768]{0:T(1024)S(1)} %copy-done.113, bf16[3072,768]{1,0:T(8,128)(2,1)} %reshape.539, f32[512,1536]{1,0:T(8,128)} %fusion.41, f32[512,1536]{1,0:T(8,128)} %fusion.45, f32[3072]{0:T(1024)S(1)} %copy-done.107), kind=kOutput, calls=%fused_computation.462 | convolution fusion | flops 2434399744 | bytes 14173184 | tf_op jit(solution)/shard_map/tf,fd->td/dot_general | solution.py:28
  295.2 4.5 all-to-all-start.2
  311.9 8.5 %reshape.546 = bf16[3072,768]{1,0:T(8,128)(2,1)} reshape(bf16[768,3072]{1,0:T(8,128)(2,1)} %pad_maximum_fusion.1) | data formatting | bytes 9437184 | tf_op jit(solution)/shard_map/reshape | solution.py:282
  320.4 7.9 all-to-all-done.2.qkv_ref
  328.3 13.6 %shard_map.212 = (bf16[4,3,64,512]{3,2,1,0:T(8,128)(2,1)}, f32[3,4,1,512]{3,2,1,0:T(1,128)S(1)}) custom-call(bf16[4,3,3,64,512]{4,3,2,1,0:T(8,128)(2,1)} %all-to-all-done.2.qkv_ref), custom_call_target="tpu_custom_call" | custom-call | flops 4026531840 | bytes 4718592 | tf_op jit(solution)/shard_map/pallas_call | solution.py:111
  351.8 5.3 all-to-all-done.3
  362.1 4.3 fusion.37
  366.5 4.9 add_convert_fusion
  371.4 7.1 convert_reduce_fusion
  395.5 9.2 %fusion.162 = f32[3072,768]{1,0:T(8,128)} fusion(bf16[512,768]{1,0:T(8,128)(2,1)S(1)} %copy-done.46, f32[512,1536]{1,0:T(8,128)S(1)} %copy-done.122, f32[512,1536]{1,0:T(8,128)} %copy-done.123, f32[3072]{0:T(1024)S(1)} %add.687), kind=kOutput, calls=%fused_computation.441 | convolution fusion | flops 2433220608 | bytes 16527360 | tf_op jit(solution)/shard_map/tf,td->fd/dot_general | solution.py:28
  407.5 25.1 %shard_map.213 = bf16[4,3,3,64,512]{4,3,2,1,0:T(8,128)(2,1)S(1)} custom-call(bf16[4,3,3,64,512]{4,3,2,1,0:T(8,128)(2,1)} %all-to-all-done.2.qkv_ref, bf16[4,3,64,512]{3,2,1,0:T(8,128)(2,1)S(1)} %all-to-all-done.4.grad_ref, f32[3,4,1,512]{3,2,1,0:T(1,128)S(1)} %get-tuple-element.52.log_ref), custom_call_target="tpu_custom_call" | custom-call | flops 10066329600 | bytes 4718592 | tf_op jit(solution)/shard_map/pallas_call | solution.py:131
  434.0 4.7 all-to-all-start.5
  440.9 7.2 fusion.186
  449.2 4.0 fusion.24
  458.2 4.1 fusion.22
  462.6 4.7 all-to-all-done.5
  479.0 7.3 convert_reduce_fusion.1
  496.7 6.8 fusion.93
  511.8 4.0 fusion.23
  529.9 4.8 fusion.185
  534.8 4.4 bitcast_add_fusion.2
  549.0 6.2 collective-permute-done.81
  576.6 24.6 %shard_map.214 = bf16[4,3,3,64,512]{4,3,2,1,0:T(8,128)(2,1)S(1)} custom-call(bf16[4,3,3,64,512]{4,3,2,1,0:T(8,128)(2,1)S(1)} %all-to-all-done.qkv_ref, bf16[4,3,64,512]{3,2,1,0:T(8,128)(2,1)S(1)} %all-to-all-done.6.grad_ref, f32[3,4,1,512]{3,2,1,0:T(1,128)S(1)} %get-tuple-element.53.log_ref), custom_call_target="tpu_custom_call" | custom-call | flops 10066329600 | bytes 4718592 | tf_op jit(solution)/shard_map/pallas_call | solution.py:131
  616.0 9.6 %collective-permute-done.107 = bf16[2,2,96,768]{3,2,1,0:T(8,128)(2,1)S(1)} collective-permute-done((bf16[2,2,96,768]{3,2,1,0:T(8,128)(2,1)S(1)}, bf16[2,2,96,768]{3,2,1,0:T(8,128)(2,1)S(1)}, u32[]{:S(2)}, u32[]{:S(2)}) %collective-permute-start.107) | collective-permute-done | bytes 589856 | tf_op jit(solution)/shard_map/ppermute | solution.py:164
  630.9 17.0 %collective-permute-done.97 = bf16[2,2,24,3072]{3,2,0,1:T(8,128)(2,1)S(1)} collective-permute-done((bf16[2,2,24,3072]{3,2,0,1:T(8,128)(2,1)S(1)}, bf16[2,2,24,3072]{3,2,0,1:T(8,128)(2,1)S(1)}, u32[]{:S(2)}, u32[]{:S(2)}) %collective-permute-start.97) | collective-permute-done | bytes 589856 | tf_op jit(solution)/shard_map/ppermute | solution.py:164
  649.1 7.2 collective-permute-done.98
  656.5 13.1 %collective-permute-done.109 = bf16[96,768]{1,0:T(8,128)(2,1)S(1)} collective-permute-done((bf16[96,768]{1,0:T(8,128)(2,1)S(1)}, bf16[96,768]{1,0:T(8,128)(2,1)S(1)}, u32[]{:S(2)}, u32[]{:S(2)}) %collective-permute-start.109) | collective-permute-done | bytes 147488 | tf_op jit(solution)/shard_map/ppermute | solution.py:164
  690.3 4.3 bitcast_add_fusion.3
  726.1 23.6 %collective-permute-done.77 = bf16[2,2,24,2304]{3,2,0,1:T(8,128)(2,1)S(1)} collective-permute-done((bf16[2,2,24,2304]{3,2,0,1:T(8,128)(2,1)S(1)}, bf16[2,2,24,2304]{3,2,0,1:T(8,128)(2,1)S(1)}, u32[]{:S(2)}, u32[]{:S(2)}) %collective-permute-start.77) | collective-permute-done | bytes 442400 | tf_op jit(solution)/shard_map/ppermute | solution.py:164
  781.9 10.3 %collective-permute-done.102 = bf16[2,2,96,768]{3,2,1,0:T(8,128)(2,1)S(1)} collective-permute-done((bf16[2,2,96,768]{3,2,1,0:T(8,128)(2,1)S(1)}, bf16[2,2,96,768]{3,2,1,0:T(8,128)(2,1)S(1)}, u32[]{:S(2)}, u32[]{:S(2)}) %collective-permute-start.102) | collective-permute-done | bytes 589856 | tf_op jit(solution)/shard_map/ppermute | solution.py:164
  794.5 8.5 %collective-permute-done.103 = bf16[2,96,768]{2,1,0:T(8,128)(2,1)S(1)} collective-permute-done((bf16[2,96,768]{2,1,0:T(8,128)(2,1)S(1)}, bf16[2,96,768]{2,1,0:T(8,128)(2,1)S(1)}, u32[]{:S(2)}, u32[]{:S(2)}) %collective-permute-start.103) | collective-permute-done | bytes 294944 | tf_op jit(solution)/shard_map/ppermute | solution.py:164
  804.3 4.0 collective-permute-done.104
  (883 shorter events, 390.1 us)
Async XLA Ops:
  10.3 22.5 %collective-permute-start.10 = (bf16[24,768]{1,0:T(8,128)(2,1)S(1)}, bf16[24,768]{1,0:T(8,128)(2,1)S(1)}, u32[]{:S(2)}, u32[]{:S(2)}) collective-permute-start(bf16[24,768]{1,0:T(8,128)(2,1)S(1)} %get-tuple-element.127), channel_id=1, source_target_pairs={{0,16},{4,20},{8,24},{12,28},{16,0},{20,4},{24,8},{28,12},{1,17},{... | collective-permute-start | bytes 110600 | tf_op jit(solution)/shard_map/ppermute | solution.py:164
  10.4 22.0 %collective-permute-start.5 = (bf16[24,768]{1,0:T(8,128)(2,1)S(1)}, bf16[24,768]{1,0:T(8,128)(2,1)S(1)}, u32[]{:S(2)}, u32[]{:S(2)}) collective-permute-start(bf16[24,768]{1,0:T(8,128)(2,1)S(1)} %get-tuple-element.128), channel_id=1, source_target_pairs={{0,2},{1,3},{2,0},{3,1},{4,6},{5,7},{6,4},{7,5},{8,10},{9,11},{10,... | collective-permute-start | bytes 110600 | tf_op jit(solution)/shard_map/ppermute | solution.py:164
  12.3 18.5 %collective-permute-start = (bf16[24,768]{1,0:T(8,128)(2,1)S(1)}, bf16[24,768]{1,0:T(8,128)(2,1)S(1)}, u32[]{:S(2)}, u32[]{:S(2)}) collective-permute-start(bf16[24,768]{1,0:T(8,128)(2,1)S(1)} %get-tuple-element.129), channel_id=1, source_target_pairs={{0,16},{4,20},{8,24},{12,28},{16,0},{20,4},{24,8},{28,12},{1,17},{... | collective-permute-start | bytes 110600 | tf_op jit(solution)/shard_map/ppermute | solution.py:164
  67.7 47.0 %all-to-all-start = ((bf16[4,3,3,64,512]{4,3,2,1,0:T(8,128)(2,1)}), bf16[4,3,3,64,512]{4,3,2,1,0:T(8,128)(2,1)S(1)}, u32[]{:S(2)}, u32[]{:S(2)}) async-start(bf16[4,3,3,64,512]{4,3,2,1,0:T(8,128)(2,1)} %pad_maximum_fusion.2), calls=%async_computation | async-start | bytes 4718592 | tf_op jit(solution)/shard_map/all_to_all | solution.py:321
  87.5 25.0 %collective-permute-start.22 = (bf16[2,2,24,2304]{3,2,1,0:T(8,128)(2,1)S(1)}, bf16[2,2,24,2304]{3,2,1,0:T(8,128)(2,1)S(1)}, u32[]{:S(2)}, u32[]{:S(2)}) collective-permute-start(bf16[2,2,24,2304]{3,2,1,0:T(8,128)(2,1)S(1)} %bitcast_dynamic-update-slice_fusion.33), channel_id=1, source_target_pairs={{0,4},{4,0},{8,12},{12,8},{16,20},{20,16},{24,28},{28,24},{1,5},{5... | collective-permute-start | bytes 1327112 | tf_op jit(solution)/shard_map/ppermute | solution.py:164
  88.7 21.1 %collective-permute-start.32 = (bf16[2,2,24,2304]{3,2,1,0:T(8,128)(2,1)S(1)}, bf16[2,2,24,2304]{3,2,1,0:T(8,128)(2,1)S(1)}, u32[]{:S(2)}, u32[]{:S(2)}) collective-permute-start(bf16[2,2,24,2304]{3,2,1,0:T(8,128)(2,1)S(1)} %bitcast_dynamic-update-slice_fusion.31), channel_id=1, source_target_pairs={{0,2},{1,3},{2,0},{3,1},{4,6},{5,7},{6,4},{7,5},{8,10},{9,11},{10,... | collective-permute-start | bytes 1327112 | tf_op jit(solution)/shard_map/ppermute | solution.py:164
  94.0 37.6 %collective-permute-start.27 = (bf16[2,2,24,2304]{3,2,1,0:T(8,128)(2,1)}, bf16[2,2,24,2304]{3,2,1,0:T(8,128)(2,1)}, u32[]{:S(2)}, u32[]{:S(2)}) collective-permute-start(bf16[2,2,24,2304]{3,2,1,0:T(8,128)(2,1)} %bitcast_dynamic-update-slice_fusion.32), channel_id=1, source_target_pairs={{0,8},{4,12},{8,0},{12,4},{16,24},{20,28},{24,16},{28,20},{1,9},{5... | collective-permute-start | bytes 1327112 | tf_op jit(solution)/shard_map/ppermute | solution.py:164
  111.5 49.7 %collective-permute-start.33 = (bf16[2,2,2,24,2304]{4,3,2,1,0:T(8,128)(2,1)}, bf16[2,2,2,24,2304]{4,3,2,1,0:T(8,128)(2,1)}, u32[]{:S(2)}, u32[]{:S(2)}) collective-permute-start(bf16[2,2,2,24,2304]{4,3,2,1,0:T(8,128)(2,1)} %bitcast_dynamic-update-slice_fusion.21), channel_id=1, source_target_pairs={{0,8},{4,12},{8,0},{12,4},{16,24},{20,28},{24,16},{28,20},{1,9},{5... | collective-permute-start | bytes 2654216 | tf_op jit(solution)/shard_map/ppermute | solution.py:164
  114.4 32.2 %collective-permute-start.23 = (bf16[2,2,2,24,2304]{4,3,2,1,0:T(8,128)(2,1)}, bf16[2,2,2,24,2304]{4,3,2,1,0:T(8,128)(2,1)}, u32[]{:S(2)}, u32[]{:S(2)}) collective-permute-start(bf16[2,2,2,24,2304]{4,3,2,1,0:T(8,128)(2,1)} %bitcast_dynamic-update-slice_fusion.23), channel_id=1, source_target_pairs={{0,2},{1,3},{2,0},{3,1},{4,6},{5,7},{6,4},{7,5},{8,10},{9,11},{10,... | collective-permute-start | bytes 2654216 | tf_op jit(solution)/shard_map/ppermute | solution.py:164
  135.4 22.3 %collective-permute-start.28 = (bf16[2,2,2,24,2304]{4,3,2,1,0:T(8,128)(2,1)}, bf16[2,2,2,24,2304]{4,3,2,1,0:T(8,128)(2,1)}, u32[]{:S(2)}, u32[]{:S(2)}) collective-permute-start(bf16[2,2,2,24,2304]{4,3,2,1,0:T(8,128)(2,1)} %bitcast_dynamic-update-slice_fusion.22), channel_id=1, source_target_pairs={{0,4},{4,0},{8,12},{12,8},{16,20},{20,16},{24,28},{28,24},{1,5},{5... | collective-permute-start | bytes 2654216 | tf_op jit(solution)/shard_map/ppermute | solution.py:164
  149.2 47.9 %collective-permute-start.24 = (bf16[2,2,2,2,24,2304]{5,4,3,2,1,0:T(8,128)(2,1)S(1)}, bf16[2,2,2,2,24,2304]{5,4,3,2,1,0:T(8,128)(2,1)S(1)}, u32[]{:S(2)}, u32[]{:S(2)}) collective-permute-start(bf16[2,2,2,2,24,2304]{5,4,3,2,1,0:T(8,128)(2,1)S(1)} %bitcast_dynamic-update-slice_fusion.13), channel_id=1, source_target_pairs={{0,1},{1,0},{2,3},{3,2},{4,5},{5,4},{6,7},{7,6},{8,9},{9,8},{10,11... | collective-permute-start | bytes 5308424 | tf_op jit(solution)/shard_map/ppermute | solution.py:164
  160.2 102.8 %collective-permute-start.29 = (bf16[2,2,2,2,24,2304]{5,4,3,2,1,0:T(8,128)(2,1)S(1)}, bf16[2,2,2,2,24,2304]{5,4,3,2,1,0:T(8,128)(2,1)S(1)}, u32[]{:S(2)}, u32[]{:S(2)}) collective-permute-start(bf16[2,2,2,2,24,2304]{5,4,3,2,1,0:T(8,128)(2,1)S(1)} %bitcast_dynamic-update-slice_fusion.12), channel_id=1, source_target_pairs={{0,1},{1,0},{2,3},{3,2},{4,5},{5,4},{6,7},{7,6},{8,9},{9,8},{10,11... | collective-permute-start | bytes 5308424 | tf_op jit(solution)/shard_map/ppermute | solution.py:164
  163.7 33.4 %collective-permute-start.34 = (bf16[2,2,2,2,24,2304]{5,4,3,2,1,0:T(8,128)(2,1)S(1)}, bf16[2,2,2,2,24,2304]{5,4,3,2,1,0:T(8,128)(2,1)S(1)}, u32[]{:S(2)}, u32[]{:S(2)}) collective-permute-start(bf16[2,2,2,2,24,2304]{5,4,3,2,1,0:T(8,128)(2,1)S(1)} %bitcast_dynamic-update-slice_fusion.11), channel_id=1, source_target_pairs={{0,1},{1,0},{2,3},{3,2},{4,5},{5,4},{6,7},{7,6},{8,9},{9,8},{10,11... | collective-permute-start | bytes 5308424 | tf_op jit(solution)/shard_map/ppermute | solution.py:164
  174.8 21.9 %collective-permute-start.38 = (bf16[2,2,2,24,2304]{4,3,2,1,0:T(8,128)(2,1)S(1)}, bf16[2,2,2,24,2304]{4,3,2,1,0:T(8,128)(2,1)S(1)}, u32[]{:S(2)}, u32[]{:S(2)}) collective-permute-start(bf16[2,2,2,24,2304]{4,3,2,1,0:T(8,128)(2,1)S(1)} %bitcast_dynamic-update-slice_fusion.20), channel_id=1, source_target_pairs={{0,2},{1,3},{2,0},{3,1},{4,6},{5,7},{6,4},{7,5},{8,10},{9,11},{10,... | collective-permute-start | bytes 2654216 | tf_op jit(solution)/shard_map/ppermute | solution.py:164
  206.3 23.7 %collective-permute-start.43 = (bf16[2,24,2304]{2,1,0:T(8,128)(2,1)S(1)}, bf16[2,24,2304]{2,1,0:T(8,128)(2,1)S(1)}, u32[]{:S(2)}, u32[]{:S(2)}) collective-permute-start(bf16[2,24,2304]{2,1,0:T(8,128)(2,1)S(1)} %bitcast_dynamic-update-slice_fusion.39), channel_id=1, source_target_pairs={{0,8},{4,12},{8,0},{12,4},{16,24},{20,28},{24,16},{28,20},{1,9},{5... | collective-permute-start | bytes 663560 | tf_op jit(solution)/shard_map/ppermute | solution.py:164
  229.2 22.6 %collective-permute-start.49 = (bf16[2,2,2,24,2304]{4,3,2,1,0:T(8,128)(2,1)S(1)}, bf16[2,2,2,24,2304]{4,3,2,1,0:T(8,128)(2,1)S(1)}, u32[]{:S(2)}, u32[]{:S(2)}) collective-permute-start(bf16[2,2,2,24,2304]{4,3,2,1,0:T(8,128)(2,1)S(1)} %bitcast_dynamic-update-slice_fusion.18), channel_id=1, source_target_pairs={{0,4},{4,0},{8,12},{12,8},{16,20},{20,16},{24,28},{28,24},{1,5},{5... | collective-permute-start | bytes 2654216 | tf_op jit(solution)/shard_map/ppermute | solution.py:164
  230.0 29.0 %collective-permute-start.44 = (bf16[2,2,24,2304]{3,2,1,0:T(8,128)(2,1)S(1)}, bf16[2,2,24,2304]{3,2,1,0:T(8,128)(2,1)S(1)}, u32[]{:S(2)}, u32[]{:S(2)}) collective-permute-start(bf16[2,2,24,2304]{3,2,1,0:T(8,128)(2,1)S(1)} %bitcast_dynamic-update-slice_fusion.29), channel_id=1, source_target_pairs={{0,4},{4,0},{8,12},{12,8},{16,20},{20,16},{24,28},{28,24},{1,5},{5... | collective-permute-start | bytes 1327112 | tf_op jit(solution)/shard_map/ppermute | solution.py:164
  231.5 29.2 %collective-permute-start.53 = (bf16[2,2,2,24,2304]{4,3,2,1,0:T(8,128)(2,1)S(1)}, bf16[2,2,2,24,2304]{4,3,2,1,0:T(8,128)(2,1)S(1)}, u32[]{:S(2)}, u32[]{:S(2)}) collective-permute-start(bf16[2,2,2,24,2304]{4,3,2,1,0:T(8,128)(2,1)S(1)} %bitcast_dynamic-update-slice_fusion.17), channel_id=1, source_target_pairs={{0,8},{4,12},{8,0},{12,4},{16,24},{20,28},{24,16},{28,20},{1,9},{5... | collective-permute-start | bytes 2654216 | tf_op jit(solution)/shard_map/ppermute | solution.py:164
  259.1 40.6 %collective-permute-start.45 = (bf16[2,2,2,24,2304]{4,3,2,1,0:T(8,128)(2,1)S(1)}, bf16[2,2,2,24,2304]{4,3,2,1,0:T(8,128)(2,1)}, u32[]{:S(2)}, u32[]{:S(2)}) collective-permute-start(bf16[2,2,2,24,2304]{4,3,2,1,0:T(8,128)(2,1)S(1)} %bitcast_dynamic-update-slice_fusion.19), channel_id=1, source_target_pairs={{0,2},{1,3},{2,0},{3,1},{4,6},{5,7},{6,4},{7,5},{8,10},{9,11},{10,... | collective-permute-start | bytes 2654216 | tf_op jit(solution)/shard_map/ppermute | solution.py:164
  263.1 42.6 %collective-permute-start.54 = (bf16[2,2,2,2,24,2304]{5,4,3,2,1,0:T(8,128)(2,1)}, bf16[2,2,2,2,24,2304]{5,4,3,2,1,0:T(8,128)(2,1)}, u32[]{:S(2)}, u32[]{:S(2)}) collective-permute-start(bf16[2,2,2,2,24,2304]{5,4,3,2,1,0:T(8,128)(2,1)} %bitcast_dynamic-update-slice_fusion.7), channel_id=1, source_target_pairs={{0,1},{1,0},{2,3},{3,2},{4,5},{5,4},{6,7},{7,6},{8,9},{9,8},{10,11... | collective-permute-start | bytes 5308424 | tf_op jit(solution)/shard_map/ppermute | solution.py:164
  295.2 33.1 %all-to-all-start.2 = ((bf16[4,3,3,64,512]{4,3,2,1,0:T(8,128)(2,1)}), bf16[4,3,3,64,512]{4,3,2,1,0:T(8,128)(2,1)}, u32[]{:S(2)}, u32[]{:S(2)}) async-start(bf16[4,3,3,64,512]{4,3,2,1,0:T(8,128)(2,1)} %pad_maximum_fusion.3), calls=%async_computation.2 | async-start | bytes 4718592 | tf_op jit(solution)/shard_map/all_to_all | solution.py:321
  303.2 42.4 %collective-permute-start.46 = (bf16[2,2,2,2,24,2304]{5,4,3,2,1,0:T(8,128)(2,1)}, bf16[2,2,2,2,24,2304]{5,4,3,2,1,0:T(8,128)(2,1)}, u32[]{:S(2)}, u32[]{:S(2)}) collective-permute-start(bf16[2,2,2,2,24,2304]{5,4,3,2,1,0:T(8,128)(2,1)} %bitcast_dynamic-update-slice_fusion.9), channel_id=1, source_target_pairs={{0,1},{1,0},{2,3},{3,2},{4,5},{5,4},{6,7},{7,6},{8,9},{9,8},{10,11... | collective-permute-start | bytes 5308424 | tf_op jit(solution)/shard_map/ppermute | solution.py:164
  388.1 19.5 %all-to-all-start.4 = ((bf16[4,3,64,512]{3,2,1,0:T(8,128)(2,1)}), bf16[4,3,64,512]{3,2,1,0:T(8,128)(2,1)S(1)}, u32[]{:S(2)}, u32[]{:S(2)}) async-start(bf16[4,3,64,512]{3,2,1,0:T(8,128)(2,1)} %bitcast.597), calls=%async_computation.4 | async-start | bytes 1572864 | tf_op jit(solution)/shard_map/all_to_all | solution.py:390
  405.9 32.9 %collective-permute-start.86 = (bf16[2,2,2,24,768]{4,3,2,1,0:T(8,128)(2,1)S(1)}, bf16[2,2,2,24,768]{4,3,2,1,0:T(8,128)(2,1)}, u32[]{:S(2)}, u32[]{:S(2)}) collective-permute-start(bf16[2,2,2,24,768]{4,3,2,1,0:T(8,128)(2,1)S(1)} %fusion.105), channel_id=1, source_target_pairs={{0,2},{1,3},{2,0},{3,1},{4,6},{5,7},{6,4},{7,5},{8,10},{9,11},{10,... | collective-permute-start | bytes 884744 | tf_op jit(solution)/shard_map/ppermute | solution.py:164
  434.0 33.3 %all-to-all-start.5 = ((bf16[4,3,3,64,512]{4,3,2,1,0:T(8,128)(2,1)}), bf16[4,3,3,64,512]{4,3,2,1,0:T(8,128)(2,1)}, u32[]{:S(2)}, u32[]{:S(2)}) async-start(bf16[4,3,3,64,512]{4,3,2,1,0:T(8,128)(2,1)} %copy-done.1), calls=%async_computation.5 | async-start | bytes 4718592 | tf_op jit(solution)/shard_map/all_to_all | solution.py:400
  454.7 61.1 %collective-permute-start.105 = (bf16[2,2,2,2,96,768]{5,4,3,0,1,2:T(8,128)(2,1)}, bf16[2,2,2,2,96,768]{5,4,3,0,1,2:T(8,128)(2,1)}, u32[]{:S(2)}, u32[]{:S(2)}) collective-permute-start(bf16[2,2,2,2,96,768]{5,4,3,0,1,2:T(8,128)(2,1)} %fusion.24), channel_id=1, source_target_pairs={{0,1},{1,0},{2,3},{3,2},{4,5},{5,4},{6,7},{7,6},{8,9},{9,8},{10,11... | collective-permute-start | bytes 7077896 | tf_op jit(solution)/shard_map/ppermute | solution.py:164
  462.3 72.4 %collective-permute-start.95 = (bf16[2,2,2,2,24,3072]{5,4,0,2,3,1:T(8,128)(2,1)}, bf16[2,2,2,2,24,3072]{5,4,0,2,3,1:T(8,128)(2,1)}, u32[]{:S(2)}, u32[]{:S(2)}) collective-permute-start(bf16[2,2,2,2,24,3072]{5,4,0,2,3,1:T(8,128)(2,1)} %fusion.22), channel_id=1, source_target_pairs={{0,1},{1,0},{2,3},{3,2},{4,5},{5,4},{6,7},{7,6},{8,9},{9,8},{10,11... | collective-permute-start | bytes 7077896 | tf_op jit(solution)/shard_map/ppermute | solution.py:164
  505.4 71.3 %all-to-all-start.6 = ((bf16[4,3,64,512]{3,2,1,0:T(8,128)(2,1)}), bf16[4,3,64,512]{3,2,1,0:T(8,128)(2,1)S(1)}, u32[]{:S(2)}, u32[]{:S(2)}) async-start(bf16[4,3,64,512]{3,2,1,0:T(8,128)(2,1)} %bitcast.596), calls=%async_computation.6 | async-start | bytes 1572864 | tf_op jit(solution)/shard_map/all_to_all | solution.py:390
  511.3 32.5 %collective-permute-start.80 = (bf16[2,2,2,2,24,768]{5,4,0,1,2,3:T(8,128)(2,1)}, bf16[2,2,2,2,24,768]{5,4,0,1,2,3:T(8,128)(2,1)}, u32[]{:S(2)}, u32[]{:S(2)}) collective-permute-start(bf16[2,2,2,2,24,768]{5,4,0,1,2,3:T(8,128)(2,1)} %fusion.88), channel_id=1, source_target_pairs={{0,1},{1,0},{2,3},{3,2},{4,5},{5,4},{6,7},{7,6},{8,9},{9,8},{10,11... | collective-permute-start | bytes 1769480 | tf_op jit(solution)/shard_map/ppermute | solution.py:164
  515.8 183.8 %collective-permute-start.100 = (bf16[2,2,2,2,96,768]{5,4,3,0,1,2:T(8,128)(2,1)}, bf16[2,2,2,2,96,768]{5,4,3,0,1,2:T(8,128)(2,1)}, u32[]{:S(2)}, u32[]{:S(2)}) collective-permute-start(bf16[2,2,2,2,96,768]{5,4,3,0,1,2:T(8,128)(2,1)} %fusion.23), channel_id=1, source_target_pairs={{0,1},{1,0},{2,3},{3,2},{4,5},{5,4},{6,7},{7,6},{8,9},{9,8},{10,11... | collective-permute-start | bytes 7077896 | tf_op jit(solution)/shard_map/ppermute | solution.py:164
  520.8 87.0 %collective-permute-start.106 = (bf16[2,2,2,96,768]{4,3,2,0,1:T(8,128)(2,1)}, bf16[2,2,2,96,768]{4,3,2,0,1:T(8,128)(2,1)}, u32[]{:S(2)}, u32[]{:S(2)}) collective-permute-start(bf16[2,2,2,96,768]{4,3,2,0,1:T(8,128)(2,1)} %fusion.72), channel_id=1, source_target_pairs={{0,4},{4,0},{8,12},{12,8},{16,20},{20,16},{24,28},{28,24},{1,5},{5... | collective-permute-start | bytes 3538952 | tf_op jit(solution)/shard_map/ppermute | solution.py:164
  529.3 96.7 %collective-permute-start.75 = (bf16[2,2,2,2,24,2304]{5,4,0,1,2,3:T(8,128)(2,1)}, bf16[2,2,2,2,24,2304]{5,4,0,1,2,3:T(8,128)(2,1)}, u32[]{:S(2)}, u32[]{:S(2)}) collective-permute-start(bf16[2,2,2,2,24,2304]{5,4,0,1,2,3:T(8,128)(2,1)} %fusion.49), channel_id=1, source_target_pairs={{0,1},{1,0},{2,3},{3,2},{4,5},{5,4},{6,7},{7,6},{8,9},{9,8},{10,11... | collective-permute-start | bytes 5308424 | tf_op jit(solution)/shard_map/ppermute | solution.py:164
  571.1 40.7 %collective-permute-start.96 = (bf16[2,2,2,24,3072]{4,3,0,1,2:T(8,128)(2,1)}, bf16[2,2,2,24,3072]{4,3,0,1,2:T(8,128)(2,1)}, u32[]{:S(2)}, u32[]{:S(2)}) collective-permute-start(bf16[2,2,2,24,3072]{4,3,0,1,2:T(8,128)(2,1)} %fusion.70), channel_id=1, source_target_pairs={{0,8},{4,12},{8,0},{12,4},{16,24},{20,28},{24,16},{28,20},{1,9},{5... | collective-permute-start | bytes 3538952 | tf_op jit(solution)/shard_map/ppermute | solution.py:164
  573.7 32.8 %collective-permute-start.84 = (bf16[24,768]{1,0:T(8,128)(2,1)S(1)}, bf16[24,768]{1,0:T(8,128)(2,1)S(1)}, u32[]{:S(2)}, u32[]{:S(2)}) collective-permute-start(bf16[24,768]{1,0:T(8,128)(2,1)S(1)} %fusion.136), channel_id=1, source_target_pairs={{0,16},{4,20},{8,24},{12,28},{16,0},{20,4},{24,8},{28,12},{1,17},{... | collective-permute-start | bytes 110600 | tf_op jit(solution)/shard_map/ppermute | solution.py:164
  602.6 68.5 %all-to-all-start.7 = ((bf16[4,3,3,64,512]{4,3,2,1,0:T(8,128)(2,1)}), bf16[4,3,3,64,512]{4,3,2,1,0:T(8,128)(2,1)S(1)}, u32[]{:S(2)}, u32[]{:S(2)}) async-start(bf16[4,3,3,64,512]{4,3,2,1,0:T(8,128)(2,1)} %copy-done), calls=%async_computation.7 | async-start | bytes 4718592 | tf_op jit(solution)/shard_map/all_to_all | solution.py:400
  606.5 82.7 %collective-permute-start.90 = (bf16[2,2,2,2,24,3072]{5,4,0,2,3,1:T(8,128)(2,1)}, bf16[2,2,2,2,24,3072]{5,4,0,2,3,1:T(8,128)(2,1)}, u32[]{:S(2)}, u32[]{:S(2)}) collective-permute-start(bf16[2,2,2,2,24,3072]{5,4,0,2,3,1:T(8,128)(2,1)} %fusion.21), channel_id=1, source_target_pairs={{0,1},{1,0},{2,3},{3,2},{4,5},{5,4},{6,7},{7,6},{8,9},{9,8},{10,11... | collective-permute-start | bytes 7077896 | tf_op jit(solution)/shard_map/ppermute | solution.py:164
  614.3 33.7 %collective-permute-start.97 = (bf16[2,2,24,3072]{3,2,0,1:T(8,128)(2,1)S(1)}, bf16[2,2,24,3072]{3,2,0,1:T(8,128)(2,1)S(1)}, u32[]{:S(2)}, u32[]{:S(2)}) collective-permute-start(bf16[2,2,24,3072]{3,2,0,1:T(8,128)(2,1)S(1)} %fusion.83), channel_id=1, source_target_pairs={{0,2},{1,3},{2,0},{3,1},{4,6},{5,7},{6,4},{7,5},{8,10},{9,11},{10,... | collective-permute-start | bytes 1769480 | tf_op jit(solution)/shard_map/ppermute | solution.py:164
  625.8 23.0 %collective-permute-start.108 = (bf16[2,96,768]{2,1,0:T(8,128)(2,1)S(1)}, bf16[2,96,768]{2,1,0:T(8,128)(2,1)S(1)}, u32[]{:S(2)}, u32[]{:S(2)}) collective-permute-start(bf16[2,96,768]{2,1,0:T(8,128)(2,1)S(1)} %fusion.109), channel_id=1, source_target_pairs={{0,16},{4,20},{8,24},{12,28},{16,0},{20,4},{24,8},{28,12},{1,17},{... | collective-permute-start | bytes 884744 | tf_op jit(solution)/shard_map/ppermute | solution.py:164
  629.0 87.6 %collective-permute-start.76 = (bf16[2,2,2,24,2304]{4,3,0,1,2:T(8,128)(2,1)}, bf16[2,2,2,24,2304]{4,3,0,1,2:T(8,128)(2,1)}, u32[]{:S(2)}, u32[]{:S(2)}) collective-permute-start(bf16[2,2,2,24,2304]{4,3,0,1,2:T(8,128)(2,1)} %fusion.77), channel_id=1, source_target_pairs={{0,2},{1,3},{2,0},{3,1},{4,6},{5,7},{6,4},{7,5},{8,10},{9,11},{10,... | collective-permute-start | bytes 2654216 | tf_op jit(solution)/shard_map/ppermute | solution.py:164
  648.9 20.7 %collective-permute-start.109 = (bf16[96,768]{1,0:T(8,128)(2,1)S(1)}, bf16[96,768]{1,0:T(8,128)(2,1)S(1)}, u32[]{:S(2)}, u32[]{:S(2)}) collective-permute-start(bf16[96,768]{1,0:T(8,128)(2,1)S(1)} %fusion.124), channel_id=1, source_target_pairs={{0,2},{1,3},{2,0},{3,1},{4,6},{5,7},{6,4},{7,5},{8,10},{9,11},{10,... | collective-permute-start | bytes 442376 | tf_op jit(solution)/shard_map/ppermute | solution.py:164
  686.9 32.5 %collective-permute-start.70 = (bf16[2,2,2,2,24,768]{5,4,0,2,3,1:T(8,128)(2,1)}, bf16[2,2,2,2,24,768]{5,4,0,2,3,1:T(8,128)(2,1)}, u32[]{:S(2)}, u32[]{:S(2)}) collective-permute-start(bf16[2,2,2,2,24,768]{5,4,0,2,3,1:T(8,128)(2,1)} %fusion.87), channel_id=1, source_target_pairs={{0,1},{1,0},{2,3},{3,2},{4,5},{5,4},{6,7},{7,6},{8,9},{9,8},{10,11... | collective-permute-start | bytes 1769480 | tf_op jit(solution)/shard_map/ppermute | solution.py:164
  689.9 32.1 %collective-permute-start.65 = (bf16[2,2,2,2,24,768]{5,4,3,0,1,2:T(8,128)(2,1)}, bf16[2,2,2,2,24,768]{5,4,3,0,1,2:T(8,128)(2,1)}, u32[]{:S(2)}, u32[]{:S(2)}) collective-permute-start(bf16[2,2,2,2,24,768]{5,4,3,0,1,2:T(8,128)(2,1)} %fusion.86), channel_id=1, source_target_pairs={{0,1},{1,0},{2,3},{3,2},{4,5},{5,4},{6,7},{7,6},{8,9},{9,8},{10,11... | collective-permute-start | bytes 1769480 | tf_op jit(solution)/shard_map/ppermute | solution.py:164
  699.5 24.5 %collective-permute-start.60 = (bf16[2,2,2,2,24,768]{5,4,3,2,1,0:T(8,128)(2,1)}, bf16[2,2,2,2,24,768]{5,4,3,2,1,0:T(8,128)(2,1)}, u32[]{:S(2)}, u32[]{:S(2)}) collective-permute-start(bf16[2,2,2,2,24,768]{5,4,3,2,1,0:T(8,128)(2,1)} %fusion.80), channel_id=1, source_target_pairs={{0,1},{1,0},{2,3},{3,2},{4,5},{5,4},{6,7},{7,6},{8,9},{9,8},{10,11... | collective-permute-start | bytes 1769480 | tf_op jit(solution)/shard_map/ppermute | solution.py:164
  711.5 65.9 %collective-permute-start.101 = (bf16[2,2,2,96,768]{4,3,2,0,1:T(8,128)(2,1)}, bf16[2,2,2,96,768]{4,3,2,0,1:T(8,128)(2,1)}, u32[]{:S(2)}, u32[]{:S(2)}) collective-permute-start(bf16[2,2,2,96,768]{4,3,2,0,1:T(8,128)(2,1)} %fusion.71), channel_id=1, source_target_pairs={{0,4},{4,0},{8,12},{12,8},{16,20},{20,16},{24,28},{28,24},{1,5},{5... | collective-permute-start | bytes 3538952 | tf_op jit(solution)/shard_map/ppermute | solution.py:164
  716.5 63.1 %collective-permute-start.91 = (bf16[2,2,2,24,3072]{4,3,0,1,2:T(8,128)(2,1)}, bf16[2,2,2,24,3072]{4,3,0,1,2:T(8,128)(2,1)S(1)}, u32[]{:S(2)}, u32[]{:S(2)}) collective-permute-start(bf16[2,2,2,24,3072]{4,3,0,1,2:T(8,128)(2,1)} %fusion.69), channel_id=1, source_target_pairs={{0,8},{4,12},{8,0},{12,4},{16,24},{20,28},{24,16},{28,20},{1,9},{5... | collective-permute-start | bytes 3538952 | tf_op jit(solution)/shard_map/ppermute | solution.py:164
  719.4 30.3 %collective-permute-start.77 = (bf16[2,2,24,2304]{3,2,0,1:T(8,128)(2,1)S(1)}, bf16[2,2,24,2304]{3,2,0,1:T(8,128)(2,1)S(1)}, u32[]{:S(2)}, u32[]{:S(2)}) collective-permute-start(bf16[2,2,24,2304]{3,2,0,1:T(8,128)(2,1)S(1)} %fusion.89), channel_id=1, source_target_pairs={{0,4},{4,0},{8,12},{12,8},{16,20},{20,16},{24,28},{28,24},{1,5},{5... | collective-permute-start | bytes 1327112 | tf_op jit(solution)/shard_map/ppermute | solution.py:164
  722.0 28.3 %collective-permute-start.71 = (bf16[2,2,2,24,768]{4,3,0,1,2:T(8,128)(2,1)S(1)}, bf16[2,2,2,24,768]{4,3,0,1,2:T(8,128)(2,1)S(1)}, u32[]{:S(2)}, u32[]{:S(2)}) collective-permute-start(bf16[2,2,2,24,768]{4,3,0,1,2:T(8,128)(2,1)S(1)} %fusion.103), channel_id=1, source_target_pairs={{0,8},{4,12},{8,0},{12,4},{16,24},{20,28},{24,16},{28,20},{1,9},{5... | collective-permute-start | bytes 884744 | tf_op jit(solution)/shard_map/ppermute | solution.py:164
  724.0 28.9 %collective-permute-start.66 = (bf16[2,2,2,24,768]{4,3,2,0,1:T(8,128)(2,1)S(1)}, bf16[2,2,2,24,768]{4,3,2,0,1:T(8,128)(2,1)S(1)}, u32[]{:S(2)}, u32[]{:S(2)}) collective-permute-start(bf16[2,2,2,24,768]{4,3,2,0,1:T(8,128)(2,1)S(1)} %fusion.102), channel_id=1, source_target_pairs={{0,4},{4,0},{8,12},{12,8},{16,20},{20,16},{24,28},{28,24},{1,5},{5... | collective-permute-start | bytes 884744 | tf_op jit(solution)/shard_map/ppermute | solution.py:164
  (210 other events, 1669.5 us)
